TPU v7x, 256 devices: a whole 4x4x8 slice. The times are simulated.
256 devices in a mesh: seq: 64 (over z, y, x_hi), head: 4 (over x_lo, core).
Axes of the slice: x: 4 (x_hi: 2, x_lo: 2; x = x_hi * 2 + x_lo), y: 4, z: 8, core: 2. Of those that a mesh axis runs over, the one named last changes fastest.
Arguments:
- inputs: bfloat16 [5376, 8192], P(None, 'seq'), may hold values from -16 to 16
- queries: bfloat16 [8192, 4096], P('seq', 'head'), may hold values from -2000 to 2000
- keys: bfloat16 [8192, 2048], P('seq', 'head'), may hold values from -6 to 6
- values: bfloat16 [8192, 2048], P('seq', 'head'), may hold values from -6 to 6
- grad_out: bfloat16 [8192, 4096], P('seq', 'head'), may hold values from -6 to 6
- doc_ids: int32 [8192], replicated, may hold values from 0 to 15, never falling along the last dimension, each value on 1 to 1024 neighbouring positions
Outputs:
- grad_queries: bfloat16 [8192, 4096], P('seq', 'head')
- grad_keys: bfloat16 [8192, 2048], P('seq', 'head')
- grad_values: bfloat16 [8192, 2048], P('seq', 'head')
- grad_key_weight: float32 [5376, 2048], P('seq', 'head')
- grad_value_weight: float32 [5376, 2048], P('seq', 'head')
Inputs may be any that keep to these rules, and one draw needn't show every extreme that they name: `doc_ids`: never falling along the sequence; each document holds at most (1024) tokens.
All inputs are finite; a program needn't handle non-finite values.
Results may differ from a plain program's by a relative error of at most 0.0053.
Values may be sent and summed in bfloat16 or wider, within the bound.
A program may use at most 128 MiB of HBM per device.

v0:
```python
import jax
import jax.numpy as jnp
from jax import lax
from jax.sharding import PartitionSpec as P

HEAD_DIM = 128
WINDOW = 1024


SCALE = 168.0 ** (-0.5)
NEG = -1e30


def passed_along(value, axis, steps):
    count = lax.axis_size(axis)
    initial, last = (max(0, -steps), min(count, count - steps))
    return lax.ppermute(value, axis, [(source, source + steps) for source in range(initial, last)])


def head_terms(q_blk, o_blk, k_blk, v_blk, allowed):
    scores = jnp.einsum("tgd,sd->gts", q_blk, k_blk, preferred_element_type=jnp.float32) * SCALE
    scores = jnp.where(allowed[None], scores, NEG)
    top = jnp.max(scores, axis=-1, keepdims=True)
    expo = jnp.exp(scores - top)
    probs_f = expo / jnp.sum(expo, axis=-1, keepdims=True)
    probs = probs_f.astype(jnp.bfloat16)
    grad_probs = jnp.einsum("tgd,sd->gts", o_blk, v_blk, preferred_element_type=jnp.float32)
    delta = jnp.sum(probs_f * grad_probs, axis=-1, keepdims=True)
    grad_scores = (SCALE * probs_f * (grad_probs - delta)).astype(jnp.bfloat16)
    grad_q = jnp.einsum("gts,sd->tgd", grad_scores, k_blk, preferred_element_type=jnp.float32)
    grad_k = jnp.einsum("gts,tgd->sd", grad_scores, q_blk, preferred_element_type=jnp.float32)
    grad_v = jnp.einsum("gts,tgd->sd", probs, o_blk, preferred_element_type=jnp.float32)
    return (grad_q, grad_k, grad_v)


def local(inputs, queries, keys, values, grad_out, doc_ids):
    rows = queries.shape[0]
    cols = keys.shape[1]
    heads_here = cols // HEAD_DIM
    group = queries.shape[1] // cols
    hops = WINDOW // rows
    span = WINDOW + rows
    shard = lax.axis_index("seq")
    key_pieces = []
    value_pieces = []
    for hop in range(hops, 0, -1):
        earlier_k, earlier_v = passed_along((keys, values), "seq", hop)
        key_pieces.append(earlier_k)
        value_pieces.append(earlier_v)
    key_window = jnp.concatenate(key_pieces + [keys], 0)
    value_window = jnp.concatenate(value_pieces + [values], 0)
    start = shard * rows
    q_pos = start + jnp.arange(rows, dtype=jnp.int32)
    k_pos = start - WINDOW + jnp.arange(span, dtype=jnp.int32)
    id_pad = jnp.concatenate([jnp.zeros((WINDOW,), jnp.int32), doc_ids])
    q_ids = lax.dynamic_slice_in_dim(doc_ids, start, rows, 0)
    k_ids = lax.dynamic_slice_in_dim(id_pad, start, span, 0)
    allowed = (k_pos[None, :] <= q_pos[:, None]) & (k_pos[None, :] > q_pos[:, None] - WINDOW)
    allowed = allowed & (k_pos[None, :] >= 0) & (k_ids[None, :] == q_ids[:, None])
    width_q = group * HEAD_DIM
    query_grads = []
    key_terms = []
    value_terms = []
    for head in range(heads_here):
        q_blk = queries[:, head * width_q : (head + 1) * width_q].reshape(rows, group, HEAD_DIM)
        o_blk = grad_out[:, head * width_q : (head + 1) * width_q].reshape(rows, group, HEAD_DIM)
        k_blk = key_window[:, head * HEAD_DIM : (head + 1) * HEAD_DIM]
        v_blk = value_window[:, head * HEAD_DIM : (head + 1) * HEAD_DIM]
        grad_q, grad_k, grad_v = head_terms(q_blk, o_blk, k_blk, v_blk, allowed)
        query_grads.append(grad_q.reshape(rows, width_q))
        key_terms.append(grad_k)
        value_terms.append(grad_v)
    grad_queries = jnp.concatenate(query_grads, 1).astype(jnp.bfloat16)
    key_term = jnp.concatenate(key_terms, 1)
    value_term = jnp.concatenate(value_terms, 1)
    key_total = key_term[WINDOW:]
    value_total = value_term[WINDOW:]
    for hop in range(1, hops + 1):
        first = (hops - hop) * rows
        sent_k = key_term[first : first + rows].astype(jnp.bfloat16)
        sent_v = value_term[first : first + rows].astype(jnp.bfloat16)
        back_k, back_v = passed_along((sent_k, sent_v), "seq", -hop)
        key_total = key_total + back_k.astype(jnp.float32)
        value_total = value_total + back_v.astype(jnp.float32)
    grad_keys = key_total.astype(jnp.bfloat16)
    grad_values = value_total.astype(jnp.bfloat16)
    both = jnp.concatenate([grad_keys, grad_values], 1)
    features = lax.all_to_all(inputs, "seq", split_axis=0, concat_axis=1, tiled=True)
    every = lax.all_gather(both, "seq", axis=0, tiled=True)
    summed = jnp.dot(features, every, preferred_element_type=jnp.float32)
    grad_key_weight = summed[:, :cols]
    grad_value_weight = summed[:, cols:]
    return (grad_queries, grad_keys, grad_values, grad_key_weight, grad_value_weight)


def solution(mesh):
    in_specs = (
        P(None, "seq"),
        P("seq", "head"),
        P("seq", "head"),
        P("seq", "head"),
        P("seq", "head"),
        P(),
    )
    out_specs = (
        P("seq", "head"),
        P("seq", "head"),
        P("seq", "head"),
        P("seq", "head"),
        P("seq", "head"),
    )
    return jax.shard_map(local, mesh=mesh, in_specs=in_specs, out_specs=out_specs, check_vma=False)
```

profile of v0, /device:TPU:4, one launch (start us, length us, event | category | flops | bytes accessed | tf_op | source)
XLA Modules:
  0.0 480.4 jit_solution(9411445102415237492)
XLA Ops:
  7.2 3.5 collective-permute-start.6
  10.7 4.8 collective-permute-start.5
  15.5 3.9 collective-permute-start.4
  19.4 5.9 %collective-permute-start.9 = (bf16[128,512]{1,0:T(8,128)(2,1)}, bf16[128,512]{1,0:T(8,128)(2,1)S(1)}, u32[]{:S(2)}, u32[]{:S(2)}) collective-permute-start(bf16[128,512]{1,0:T(8,128)(2,1)} %param.9), channel_id=1, source_target_pairs={{0,28},{4,32},{8,36},{12,40},{16,44},{20,48},{24,52},{28,56},{32,6... | collective-permute-start | bytes 393224 | tf_op jit(solution)/shard_map/ppermute | solution.py:17
  25.3 3.8 collective-permute-start.8
  31.7 1.1 compare_and_fusion
  32.7 1.0 fusion.58
  38.4 4.3 collective-permute-start.10
  42.7 6.1 %collective-permute-start.11 = (bf16[128,512]{1,0:T(8,128)(2,1)S(1)}, bf16[128,512]{1,0:T(8,128)(2,1)S(1)}, u32[]{:S(2)}, u32[]{:S(2)}) collective-permute-start(bf16[128,512]{1,0:T(8,128)(2,1)S(1)} %copy-done.16), channel_id=1, source_target_pairs={{0,20},{4,24},{8,28},{12,32},{16,36},{20,40},{24,44},{28,48},{32,5... | collective-permute-start | bytes 393224 | tf_op jit(solution)/shard_map/ppermute | solution.py:17
  48.8 3.9 collective-permute-start.12
  52.8 6.1 %collective-permute-start.13 = (bf16[128,512]{1,0:T(8,128)(2,1)S(1)}, bf16[128,512]{1,0:T(8,128)(2,1)S(1)}, u32[]{:S(2)}, u32[]{:S(2)}) collective-permute-start(bf16[128,512]{1,0:T(8,128)(2,1)S(1)} %copy-done.16), channel_id=1, source_target_pairs={{0,12},{4,16},{8,20},{12,24},{16,28},{20,32},{24,36},{28,40},{32,4... | collective-permute-start | bytes 393224 | tf_op jit(solution)/shard_map/ppermute | solution.py:17
  58.9 4.2 collective-permute-start.14
  63.2 2.8 collective-permute-start.15
  66.0 12.6 %collective-permute-start.1 = (bf16[128,512]{1,0:T(8,128)(2,1)S(1)}, bf16[128,512]{1,0:T(8,128)(2,1)S(1)}, u32[]{:S(2)}, u32[]{:S(2)}) collective-permute-start(bf16[128,512]{1,0:T(8,128)(2,1)S(1)} %copy-done.17), channel_id=1, source_target_pairs={{0,28},{4,32},{8,36},{12,40},{16,44},{20,48},{24,52},{28,56},{32,6... | collective-permute-start | bytes 393224 | tf_op jit(solution)/shard_map/ppermute | solution.py:17
  78.6 3.4 collective-permute-start
  82.1 2.4 collective-permute-done
  84.5 1.3 collective-permute-start.2
  85.9 5.6 %collective-permute-start.3 = (bf16[128,512]{1,0:T(8,128)(2,1)S(1)}, bf16[128,512]{1,0:T(8,128)(2,1)S(1)}, u32[]{:S(2)}, u32[]{:S(2)}) collective-permute-start(bf16[128,512]{1,0:T(8,128)(2,1)S(1)} %copy-done.17), channel_id=1, source_target_pairs={{0,20},{4,24},{8,28},{12,32},{16,36},{20,40},{24,44},{28,48},{32,5... | collective-permute-start | bytes 393224 | tf_op jit(solution)/shard_map/ppermute | solution.py:17
  91.5 4.5 collective-permute-start.7
  96.2 3.7 collective-permute-done.7
  100.6 1.9 convolution_bitcast_fusion.7
  102.4 1.4 multiply_reduce_fusion.3
  104.3 1.6 fusion.61
  105.9 2.8 convolution_bitcast_fusion.6
  108.8 1.4 multiply_reduce_fusion.2
  111.9 2.5 fusion.60
  114.5 2.8 convolution_bitcast_fusion.5
  117.3 1.9 multiply_reduce_fusion.1
  120.4 2.6 fusion.59
  123.0 2.9 convolution_bitcast_fusion.4
  125.9 1.9 multiply_reduce_fusion
  129.7 2.1 collective-permute-start.16
  131.8 1.3 collective-permute-start.23
  133.1 1.3 collective-permute-start.22
  134.4 1.3 collective-permute-start.21
  135.7 1.5 collective-permute-start.20
  137.3 3.2 collective-permute-done.16
  140.5 1.3 collective-permute-start.19
  142.0 4.0 collective-permute-done.23
  146.0 1.3 collective-permute-start.18
  147.3 2.1 collective-permute-done.22
  149.4 1.3 collective-permute-start.17
  150.7 1.9 collective-permute-start.24
  152.7 1.3 collective-permute-start.31
  154.0 1.3 collective-permute-start.30
  155.5 3.3 collective-permute-done.18
  158.8 1.3 collective-permute-start.29
  160.1 1.3 collective-permute-start.28
  162.3 1.3 collective-permute-start.27
  164.5 1.3 collective-permute-start.26
  165.8 5.3 %collective-permute-done.30 = bf16[128,512]{0,1:T(8,128)(2,1)S(1)} collective-permute-done((bf16[128,512]{0,1:T(8,128)(2,1)S(1)}, bf16[128,512]{0,1:T(8,128)(2,1)S(1)}, u32[]{:S(2)}, u32[]{:S(2)}) %collective-permute-start.30) | collective-permute-done | bytes 131104 | tf_op jit(solution)/shard_map/ppermute | solution.py:17
  171.0 1.3 collective-permute-start.25
  172.7 3.0 collective-permute-done.26
  175.7 2.2 collective-permute-done.25
  178.8 1.3 all_to_all.14
  180.1 31.3 %all-to-all-start = ((bf16[64,84,128]{2,1,0:T(8,128)(2,1)}), bf16[64,84,128]{2,1,0:T(8,128)(2,1)S(1)}, u32[]{:S(2)}, u32[]{:S(2)}) async-start(bf16[64,84,128]{2,1,0:T(8,128)(2,1)} %all_to_all.14), calls=%async_computation | async-start | bytes 2883584 | tf_op jit(solution)/shard_map/all_to_all | solution.py:88
  211.4 1.9 convolution_convert_fusion.3
  214.3 1.9 convolution_convert_fusion.2
  217.1 1.2 convolution_convert_fusion.1
  218.5 1.2 convolution_convert_fusion
  222.1 13.1 %all-to-all-done = bf16[64,84,128]{2,1,0:T(8,128)(2,1)S(1)} async-done(((bf16[64,84,128]{2,1,0:T(8,128)(2,1)}), bf16[64,84,128]{2,1,0:T(8,128)(2,1)S(1)}, u32[]{:S(2)}, u32[]{:S(2)}) %all-to-all-start) | async-done | bytes 1376288 | tf_op jit(solution)/shard_map/all_to_all | solution.py:88
  235.7 1.1 copy.116
  236.8 225.0 %all-gather.2.cloned.1.call-done = bf16[8192,1024]{0,1:T(8,128)(2,1)} async-done(((bf16[128,1024]{0,1:T(8,128)(2,1)}), bf16[8192,1024]{0,1:T(8,128)(2,1)}) %all-gather.2.cloned.1.call-update) | async-done | bytes 16777232 | tf_op jit(solution)/shard_map/all_gather | solution.py:89
  461.8 11.0 %convolution_bitcast_fusion.12 = f32[84,1024]{1,0:T(8,128)S(1)} fusion(bf16[8192,1024]{0,1:T(8,128)(2,1)} %all-gather.2.cloned.1.call-done, bf16[84,8192]{1,0:T(8,128)(2,1)S(1)} %bitcast.218), kind=kOutput, calls=%fused_computation.38 | convolution fusion | flops 1409286144 | bytes 18497536 | tf_op jit(solution)/shard_map/dot_general | solution.py:90
  (124 shorter events, 22.6 us)
Async XLA Ops:
  7.2 454.6 %all-gather.2.cloned.1.call-start = ((), (), s32[]{:S(2)}) async-start(), calls=%async_computation.1 | async-start | bytes 17039360 | tf_op jit(solution)/shard_map/all_gather | solution.py:89
  7.2 89.0 %collective-permute-start.6 = (bf16[128,512]{1,0:T(8,128)(2,1)}, bf16[128,512]{1,0:T(8,128)(2,1)S(1)}, u32[]{:S(2)}, u32[]{:S(2)}) collective-permute-start(bf16[128,512]{1,0:T(8,128)(2,1)} %param.8), channel_id=1, source_target_pairs={{0,8},{4,12},{8,16},{12,20},{16,24},{20,28},{24,32},{28,36},{32,40... | collective-permute-start | bytes 393224 | tf_op jit(solution)/shard_map/ppermute | solution.py:17
  10.7 85.4 %collective-permute-start.5 = (bf16[128,512]{1,0:T(8,128)(2,1)}, bf16[128,512]{1,0:T(8,128)(2,1)S(1)}, u32[]{:S(2)}, u32[]{:S(2)}) collective-permute-start(bf16[128,512]{1,0:T(8,128)(2,1)} %param.8), channel_id=1, source_target_pairs={{0,12},{4,16},{8,20},{12,24},{16,28},{20,32},{24,36},{28,40},{32,4... | collective-permute-start | bytes 393224 | tf_op jit(solution)/shard_map/ppermute | solution.py:17
  15.5 80.6 %collective-permute-start.4 = (bf16[128,512]{1,0:T(8,128)(2,1)}, bf16[128,512]{1,0:T(8,128)(2,1)S(1)}, u32[]{:S(2)}, u32[]{:S(2)}) collective-permute-start(bf16[128,512]{1,0:T(8,128)(2,1)} %param.8), channel_id=1, source_target_pairs={{0,16},{4,20},{8,24},{12,28},{16,32},{20,36},{24,40},{28,44},{32,4... | collective-permute-start | bytes 393224 | tf_op jit(solution)/shard_map/ppermute | solution.py:17
  19.4 23.4 %collective-permute-start.9 = (bf16[128,512]{1,0:T(8,128)(2,1)}, bf16[128,512]{1,0:T(8,128)(2,1)S(1)}, u32[]{:S(2)}, u32[]{:S(2)}) collective-permute-start(bf16[128,512]{1,0:T(8,128)(2,1)} %param.9), channel_id=1, source_target_pairs={{0,28},{4,32},{8,36},{12,40},{16,44},{20,48},{24,52},{28,56},{32,6... | collective-permute-start | bytes 393224 | tf_op jit(solution)/shard_map/ppermute | solution.py:17
  25.3 13.1 %collective-permute-start.8 = (bf16[128,512]{1,0:T(8,128)(2,1)}, bf16[128,512]{1,0:T(8,128)(2,1)S(1)}, u32[]{:S(2)}, u32[]{:S(2)}) collective-permute-start(bf16[128,512]{1,0:T(8,128)(2,1)} %param.9), channel_id=1, source_target_pairs={{0,32},{4,36},{8,40},{12,44},{16,48},{20,52},{24,56},{28,60},{32,6... | collective-permute-start | bytes 393224 | tf_op jit(solution)/shard_map/ppermute | solution.py:17
  29.1 9.3 %copy-start.16 = (bf16[128,512]{1,0:T(8,128)(2,1)S(1)}, bf16[128,512]{1,0:T(8,128)(2,1)}, u32[]{:S(2)}) copy-start(bf16[128,512]{1,0:T(8,128)(2,1)} %param.9) | copy-start | bytes 393220
  32.7 67.8 %copy-start.14 = (pred[128,1152]{0,1:T(8,128)(4,1)}, pred[128,1152]{0,1:T(8,128)(4,1)S(1)}, u32[]{:S(2)}) copy-start(pred[128,1152]{0,1:T(8,128)(4,1)S(1)} %compare_and_fusion) | copy-start | bytes 442372
  34.6 31.4 %copy-start.17 = (bf16[128,512]{1,0:T(8,128)(2,1)S(1)}, bf16[128,512]{1,0:T(8,128)(2,1)}, u32[]{:S(2)}) copy-start(bf16[128,512]{1,0:T(8,128)(2,1)} %param.8) | copy-start | bytes 393220
  38.4 10.4 %collective-permute-start.10 = (bf16[128,512]{1,0:T(8,128)(2,1)S(1)}, bf16[128,512]{1,0:T(8,128)(2,1)S(1)}, u32[]{:S(2)}, u32[]{:S(2)}) collective-permute-start(bf16[128,512]{1,0:T(8,128)(2,1)S(1)} %copy-done.16), channel_id=1, source_target_pairs={{0,24},{4,28},{8,32},{12,36},{16,40},{20,44},{24,48},{28,52},{32,5... | collective-permute-start | bytes 393224 | tf_op jit(solution)/shard_map/ppermute | solution.py:17
  42.7 10.0 %collective-permute-start.11 = (bf16[128,512]{1,0:T(8,128)(2,1)S(1)}, bf16[128,512]{1,0:T(8,128)(2,1)S(1)}, u32[]{:S(2)}, u32[]{:S(2)}) collective-permute-start(bf16[128,512]{1,0:T(8,128)(2,1)S(1)} %copy-done.16), channel_id=1, source_target_pairs={{0,20},{4,24},{8,28},{12,32},{16,36},{20,40},{24,44},{28,48},{32,5... | collective-permute-start | bytes 393224 | tf_op jit(solution)/shard_map/ppermute | solution.py:17
  48.8 10.1 %collective-permute-start.12 = (bf16[128,512]{1,0:T(8,128)(2,1)S(1)}, bf16[128,512]{1,0:T(8,128)(2,1)S(1)}, u32[]{:S(2)}, u32[]{:S(2)}) collective-permute-start(bf16[128,512]{1,0:T(8,128)(2,1)S(1)} %copy-done.16), channel_id=1, source_target_pairs={{0,16},{4,20},{8,24},{12,28},{16,32},{20,36},{24,40},{28,44},{32,4... | collective-permute-start | bytes 393224 | tf_op jit(solution)/shard_map/ppermute | solution.py:17
  52.8 10.4 %collective-permute-start.13 = (bf16[128,512]{1,0:T(8,128)(2,1)S(1)}, bf16[128,512]{1,0:T(8,128)(2,1)S(1)}, u32[]{:S(2)}, u32[]{:S(2)}) collective-permute-start(bf16[128,512]{1,0:T(8,128)(2,1)S(1)} %copy-done.16), channel_id=1, source_target_pairs={{0,12},{4,16},{8,20},{12,24},{16,28},{20,32},{24,36},{28,40},{32,4... | collective-permute-start | bytes 393224 | tf_op jit(solution)/shard_map/ppermute | solution.py:17
  58.9 7.0 %collective-permute-start.14 = (bf16[128,512]{1,0:T(8,128)(2,1)S(1)}, bf16[128,512]{1,0:T(8,128)(2,1)S(1)}, u32[]{:S(2)}, u32[]{:S(2)}) collective-permute-start(bf16[128,512]{1,0:T(8,128)(2,1)S(1)} %copy-done.16), channel_id=1, source_target_pairs={{0,8},{4,12},{8,16},{12,20},{16,24},{20,28},{24,32},{28,36},{32,40... | collective-permute-start | bytes 393224 | tf_op jit(solution)/shard_map/ppermute | solution.py:17
  63.2 15.5 %collective-permute-start.15 = (bf16[128,512]{1,0:T(8,128)(2,1)S(1)}, bf16[128,512]{1,0:T(8,128)(2,1)S(1)}, u32[]{:S(2)}, u32[]{:S(2)}) collective-permute-start(bf16[128,512]{1,0:T(8,128)(2,1)S(1)} %copy-done.16), channel_id=1, source_target_pairs={{0,4},{4,8},{8,12},{12,16},{16,20},{20,24},{24,28},{28,32},{32,36}... | collective-permute-start | bytes 393224 | tf_op jit(solution)/shard_map/ppermute | solution.py:17
  66.0 19.9 %collective-permute-start.1 = (bf16[128,512]{1,0:T(8,128)(2,1)S(1)}, bf16[128,512]{1,0:T(8,128)(2,1)S(1)}, u32[]{:S(2)}, u32[]{:S(2)}) collective-permute-start(bf16[128,512]{1,0:T(8,128)(2,1)S(1)} %copy-done.17), channel_id=1, source_target_pairs={{0,28},{4,32},{8,36},{12,40},{16,44},{20,48},{24,52},{28,56},{32,6... | collective-permute-start | bytes 393224 | tf_op jit(solution)/shard_map/ppermute | solution.py:17
  78.6 5.9 %collective-permute-start = (bf16[128,512]{1,0:T(8,128)(2,1)S(1)}, bf16[128,512]{1,0:T(8,128)(2,1)S(1)}, u32[]{:S(2)}, u32[]{:S(2)}) collective-permute-start(bf16[128,512]{1,0:T(8,128)(2,1)S(1)} %copy-done.17), channel_id=1, source_target_pairs={{0,32},{4,36},{8,40},{12,44},{16,48},{20,52},{24,56},{28,60},{32,6... | collective-permute-start | bytes 393224 | tf_op jit(solution)/shard_map/ppermute | solution.py:17
  82.1 17.8 %copy-start.19 = (bf16[1152,512]{1,0:T(8,128)(2,1)}, bf16[1152,512]{1,0:T(8,128)(2,1)S(1)}, u32[]{:S(2)}) copy-start(bf16[1152,512]{1,0:T(8,128)(2,1)S(1)} %constant_dynamic-update-slice_fusion.9) | copy-start | bytes 3538948
  84.5 7.0 %collective-permute-start.2 = (bf16[128,512]{1,0:T(8,128)(2,1)S(1)}, bf16[128,512]{1,0:T(8,128)(2,1)S(1)}, u32[]{:S(2)}, u32[]{:S(2)}) collective-permute-start(bf16[128,512]{1,0:T(8,128)(2,1)S(1)} %copy-done.17), channel_id=1, source_target_pairs={{0,24},{4,28},{8,32},{12,36},{16,40},{20,44},{24,48},{28,52},{32,5... | collective-permute-start | bytes 393224 | tf_op jit(solution)/shard_map/ppermute | solution.py:17
  85.9 10.2 %collective-permute-start.3 = (bf16[128,512]{1,0:T(8,128)(2,1)S(1)}, bf16[128,512]{1,0:T(8,128)(2,1)S(1)}, u32[]{:S(2)}, u32[]{:S(2)}) collective-permute-start(bf16[128,512]{1,0:T(8,128)(2,1)S(1)} %copy-done.17), channel_id=1, source_target_pairs={{0,20},{4,24},{8,28},{12,32},{16,36},{20,40},{24,44},{28,48},{32,5... | collective-permute-start | bytes 393224 | tf_op jit(solution)/shard_map/ppermute | solution.py:17
  91.5 8.4 %collective-permute-start.7 = (bf16[128,512]{1,0:T(8,128)(2,1)S(1)}, bf16[128,512]{1,0:T(8,128)(2,1)S(1)}, u32[]{:S(2)}, u32[]{:S(2)}) collective-permute-start(bf16[128,512]{1,0:T(8,128)(2,1)S(1)} %copy-done.17), channel_id=1, source_target_pairs={{0,4},{4,8},{8,12},{12,16},{16,20},{20,24},{24,28},{28,32},{32,36}... | collective-permute-start | bytes 393224 | tf_op jit(solution)/shard_map/ppermute | solution.py:17
  99.9 6.0 %copy-start.6 = (bf16[1152,512]{1,0:T(8,128)(2,1)}, bf16[1152,512]{1,0:T(8,128)(2,1)S(1)}, u32[]{:S(2)}) copy-start(bf16[1152,512]{1,0:T(8,128)(2,1)S(1)} %constant_dynamic-update-slice_fusion) | copy-start | bytes 3538948
  110.1 0.8 copy-start.13
  111.0 0.8 copy-start.11
  111.0 0.9 copy-start.15
  111.9 2.5 copy-start.18
  117.3 1.9 copy-start.9
  119.2 0.8 copy-start.12
  125.9 1.9 copy-start.8
  127.8 1.0 copy-start.10
  128.0 0.8 copy-start
  129.3 7.9 %copy-start.5 = (f32[1152,128]{0,1:T(8,128)S(1)}, f32[1152,128]{0,1:T(8,128)}, u32[]{:S(2)}) copy-start(f32[1152,128]{0,1:T(8,128)} %convolution_bitcast_fusion.4) | copy-start | bytes 1769476
  129.5 7.7 %copy-start.2 = (f32[1152,128]{0,1:T(8,128)S(1)}, f32[1152,128]{0,1:T(8,128)}, u32[]{:S(2)}) copy-start(f32[1152,128]{0,1:T(8,128)} %convolution_bitcast_fusion.7) | copy-start | bytes 1769476
  129.5 7.7 %copy-start.3 = (f32[1152,128]{0,1:T(8,128)S(1)}, f32[1152,128]{0,1:T(8,128)}, u32[]{:S(2)}) copy-start(f32[1152,128]{0,1:T(8,128)} %convolution_bitcast_fusion.6) | copy-start | bytes 1769476
  129.5 7.7 %copy-start.4 = (f32[1152,128]{0,1:T(8,128)S(1)}, f32[1152,128]{0,1:T(8,128)}, u32[]{:S(2)}) copy-start(f32[1152,128]{0,1:T(8,128)} %convolution_bitcast_fusion.5) | copy-start | bytes 1769476
  129.7 10.8 %collective-permute-start.16 = (bf16[128,512]{0,1:T(8,128)(2,1)S(1)}, bf16[128,512]{0,1:T(8,128)(2,1)S(1)}, u32[]{:S(2)}, u32[]{:S(2)}) collective-permute-start(bf16[128,512]{0,1:T(8,128)(2,1)S(1)} %get-tuple-element.23), channel_id=1, source_target_pairs={{4,0},{8,4},{12,8},{16,12},{20,16},{24,20},{28,24},{32,28},{36,32}... | collective-permute-start | bytes 393224 | tf_op jit(solution)/shard_map/ppermute | solution.py:17
  131.8 14.2 %collective-permute-start.23 = (bf16[128,512]{0,1:T(8,128)(2,1)S(1)}, bf16[128,512]{0,1:T(8,128)(2,1)S(1)}, u32[]{:S(2)}, u32[]{:S(2)}) collective-permute-start(bf16[128,512]{0,1:T(8,128)(2,1)S(1)} %get-tuple-element.24), channel_id=1, source_target_pairs={{32,0},{36,4},{40,8},{44,12},{48,16},{52,20},{56,24},{60,28},{64,3... | collective-permute-start | bytes 393224 | tf_op jit(solution)/shard_map/ppermute | solution.py:17
  133.1 16.4 %collective-permute-start.22 = (bf16[128,512]{0,1:T(8,128)(2,1)S(1)}, bf16[128,512]{0,1:T(8,128)(2,1)S(1)}, u32[]{:S(2)}, u32[]{:S(2)}) collective-permute-start(bf16[128,512]{0,1:T(8,128)(2,1)S(1)} %get-tuple-element.25), channel_id=1, source_target_pairs={{28,0},{32,4},{36,8},{40,12},{44,16},{48,20},{52,24},{56,28},{60,3... | collective-permute-start | bytes 393224 | tf_op jit(solution)/shard_map/ppermute | solution.py:17
  134.4 16.3 %collective-permute-start.21 = (bf16[128,512]{0,1:T(8,128)(2,1)S(1)}, bf16[128,512]{0,1:T(8,128)(2,1)S(1)}, u32[]{:S(2)}, u32[]{:S(2)}) collective-permute-start(bf16[128,512]{0,1:T(8,128)(2,1)S(1)} %get-tuple-element.26), channel_id=1, source_target_pairs={{24,0},{28,4},{32,8},{36,12},{40,16},{44,20},{48,24},{52,28},{56,3... | collective-permute-start | bytes 393224 | tf_op jit(solution)/shard_map/ppermute | solution.py:17
  135.7 17.0 %collective-permute-start.20 = (bf16[128,512]{0,1:T(8,128)(2,1)S(1)}, bf16[128,512]{0,1:T(8,128)(2,1)S(1)}, u32[]{:S(2)}, u32[]{:S(2)}) collective-permute-start(bf16[128,512]{0,1:T(8,128)(2,1)S(1)} %get-tuple-element.27), channel_id=1, source_target_pairs={{20,0},{24,4},{28,8},{32,12},{36,16},{40,20},{44,24},{48,28},{52,3... | collective-permute-start | bytes 393224 | tf_op jit(solution)/shard_map/ppermute | solution.py:17
  140.5 13.5 %collective-permute-start.19 = (bf16[128,512]{0,1:T(8,128)(2,1)S(1)}, bf16[128,512]{0,1:T(8,128)(2,1)S(1)}, u32[]{:S(2)}, u32[]{:S(2)}) collective-permute-start(bf16[128,512]{0,1:T(8,128)(2,1)S(1)} %get-tuple-element.28), channel_id=1, source_target_pairs={{16,0},{20,4},{24,8},{28,12},{32,16},{36,20},{40,24},{44,28},{48,3... | collective-permute-start | bytes 393224 | tf_op jit(solution)/shard_map/ppermute | solution.py:17
  146.0 12.8 %collective-permute-start.18 = (bf16[128,512]{0,1:T(8,128)(2,1)S(1)}, bf16[128,512]{0,1:T(8,128)(2,1)S(1)}, u32[]{:S(2)}, u32[]{:S(2)}) collective-permute-start(bf16[128,512]{0,1:T(8,128)(2,1)S(1)} %get-tuple-element.29), channel_id=1, source_target_pairs={{12,0},{16,4},{20,8},{24,12},{28,16},{32,20},{36,24},{40,28},{44,3... | collective-permute-start | bytes 393224 | tf_op jit(solution)/shard_map/ppermute | solution.py:17
  149.4 10.6 %collective-permute-start.17 = (bf16[128,512]{0,1:T(8,128)(2,1)S(1)}, bf16[128,512]{0,1:T(8,128)(2,1)S(1)}, u32[]{:S(2)}, u32[]{:S(2)}) collective-permute-start(bf16[128,512]{0,1:T(8,128)(2,1)S(1)} %get-tuple-element.30), channel_id=1, source_target_pairs={{8,0},{12,4},{16,8},{20,12},{24,16},{28,20},{32,24},{36,28},{40,32... | collective-permute-start | bytes 393224 | tf_op jit(solution)/shard_map/ppermute | solution.py:17
  150.7 11.6 %collective-permute-start.24 = (bf16[128,512]{0,1:T(8,128)(2,1)S(1)}, bf16[128,512]{0,1:T(8,128)(2,1)S(1)}, u32[]{:S(2)}, u32[]{:S(2)}) collective-permute-start(bf16[128,512]{0,1:T(8,128)(2,1)S(1)} %get-tuple-element.15), channel_id=1, source_target_pairs={{4,0},{8,4},{12,8},{16,12},{20,16},{24,20},{28,24},{32,28},{36,32}... | collective-permute-start | bytes 393224 | tf_op jit(solution)/shard_map/ppermute | solution.py:17
  152.7 11.8 %collective-permute-start.31 = (bf16[128,512]{0,1:T(8,128)(2,1)S(1)}, bf16[128,512]{0,1:T(8,128)(2,1)S(1)}, u32[]{:S(2)}, u32[]{:S(2)}) collective-permute-start(bf16[128,512]{0,1:T(8,128)(2,1)S(1)} %get-tuple-element.16), channel_id=1, source_target_pairs={{32,0},{36,4},{40,8},{44,12},{48,16},{52,20},{56,24},{60,28},{64,3... | collective-permute-start | bytes 393224 | tf_op jit(solution)/shard_map/ppermute | solution.py:17
  154.0 17.0 %collective-permute-start.30 = (bf16[128,512]{0,1:T(8,128)(2,1)S(1)}, bf16[128,512]{0,1:T(8,128)(2,1)S(1)}, u32[]{:S(2)}, u32[]{:S(2)}) collective-permute-start(bf16[128,512]{0,1:T(8,128)(2,1)S(1)} %get-tuple-element.17), channel_id=1, source_target_pairs={{28,0},{32,4},{36,8},{40,12},{44,16},{48,20},{52,24},{56,28},{60,3... | collective-permute-start | bytes 393224 | tf_op jit(solution)/shard_map/ppermute | solution.py:17
  158.8 13.7 %collective-permute-start.29 = (bf16[128,512]{0,1:T(8,128)(2,1)S(1)}, bf16[128,512]{0,1:T(8,128)(2,1)S(1)}, u32[]{:S(2)}, u32[]{:S(2)}) collective-permute-start(bf16[128,512]{0,1:T(8,128)(2,1)S(1)} %get-tuple-element.18), channel_id=1, source_target_pairs={{24,0},{28,4},{32,8},{36,12},{40,16},{44,20},{48,24},{52,28},{56,3... | collective-permute-start | bytes 393224 | tf_op jit(solution)/shard_map/ppermute | solution.py:17
  160.1 12.4 %collective-permute-start.28 = (bf16[128,512]{0,1:T(8,128)(2,1)S(1)}, bf16[128,512]{0,1:T(8,128)(2,1)S(1)}, u32[]{:S(2)}, u32[]{:S(2)}) collective-permute-start(bf16[128,512]{0,1:T(8,128)(2,1)S(1)} %get-tuple-element.19), channel_id=1, source_target_pairs={{20,0},{24,4},{28,8},{32,12},{36,16},{40,20},{44,24},{48,28},{52,3... | collective-permute-start | bytes 393224 | tf_op jit(solution)/shard_map/ppermute | solution.py:17
  162.3 10.4 %collective-permute-start.27 = (bf16[128,512]{0,1:T(8,128)(2,1)S(1)}, bf16[128,512]{0,1:T(8,128)(2,1)S(1)}, u32[]{:S(2)}, u32[]{:S(2)}) collective-permute-start(bf16[128,512]{0,1:T(8,128)(2,1)S(1)} %get-tuple-element.20), channel_id=1, source_target_pairs={{16,0},{20,4},{24,8},{28,12},{32,16},{36,20},{40,24},{44,28},{48,3... | collective-permute-start | bytes 393224 | tf_op jit(solution)/shard_map/ppermute | solution.py:17
  164.5 11.2 %collective-permute-start.26 = (bf16[128,512]{0,1:T(8,128)(2,1)S(1)}, bf16[128,512]{0,1:T(8,128)(2,1)S(1)}, u32[]{:S(2)}, u32[]{:S(2)}) collective-permute-start(bf16[128,512]{0,1:T(8,128)(2,1)S(1)} %get-tuple-element.21), channel_id=1, source_target_pairs={{12,0},{16,4},{20,8},{24,12},{28,16},{32,20},{36,24},{40,28},{44,3... | collective-permute-start | bytes 393224 | tf_op jit(solution)/shard_map/ppermute | solution.py:17
  171.0 6.8 %collective-permute-start.25 = (bf16[128,512]{0,1:T(8,128)(2,1)S(1)}, bf16[128,512]{0,1:T(8,128)(2,1)S(1)}, u32[]{:S(2)}, u32[]{:S(2)}) collective-permute-start(bf16[128,512]{0,1:T(8,128)(2,1)S(1)} %get-tuple-element.22), channel_id=1, source_target_pairs={{8,0},{12,4},{16,8},{20,12},{24,16},{28,20},{32,24},{36,28},{40,32... | collective-permute-start | bytes 393224 | tf_op jit(solution)/shard_map/ppermute | solution.py:17
  172.5 6.3 %copy-start.7 = (bf16[5376,128]{1,0:T(8,128)(2,1)S(1)}, bf16[5376,128]{1,0:T(8,128)(2,1)}, u32[]{:S(2)}) copy-start(bf16[5376,128]{1,0:T(8,128)(2,1)} %param.6) | copy-start | bytes 4128772
  180.1 55.1 %all-to-all-start = ((bf16[64,84,128]{2,1,0:T(8,128)(2,1)}), bf16[64,84,128]{2,1,0:T(8,128)(2,1)S(1)}, u32[]{:S(2)}, u32[]{:S(2)}) async-start(bf16[64,84,128]{2,1,0:T(8,128)(2,1)} %all_to_all.14), calls=%async_computation | async-start | bytes 2883584 | tf_op jit(solution)/shard_map/all_to_all | solution.py:88
  213.3 5.2 %copy-start.1 = (bf16[2,128,1152]{1,2,0:T(8,128)(2,1)S(1)}, bf16[2,128,1152]{1,2,0:T(8,128)(2,1)}, u32[]{:S(2)}) copy-start(bf16[2,128,1152]{1,2,0:T(8,128)(2,1)} %copy-done) | copy-start | bytes 1769476
Sparse Core Ops, SparseCore 0:
  178.9 282.8 all-gather.1
where the time goes:
time: 485 us; the launch traced here: 480 us
  waiting for transfers between devices  269 us (55%)
  starting transfers between devices  130 us (27%)
  matrix products  42.9 us (9%)
  local copies, waits for them, and re-layouts  18 us (4%)
  between operations  15 us (3%)
  other arithmetic  4.99 us (1%)
    all_gather x1, waiting for transfers between devices, local(): every = lax.all_gather(both, 'seq', axis=0, tiled=True)  225 us
    ppermute x32, starting transfers between devices, passed_along(): lax.ppermute(value, axis, [(source, source + steps) for source in range(i...  98.8 us
    all_to_all x1, starting transfers between devices, local(): lax.all_to_all(inputs, 'seq', split_axis=0, concat_axis=1, tiled=True)  31.3 us
    ppermute x32, waiting for transfers between devices, passed_along(): lax.ppermute(value, axis, [(source, source + steps) for source in range(i...  31.3 us
    all_to_all x1, waiting for transfers between devices, local(): lax.all_to_all(inputs, 'seq', split_axis=0, concat_axis=1, tiled=True)  13.1 us
    dot_general x1, matrix products, local(): summed = jnp.dot(features, every, preferred_element_type=jnp.float32)  11 us
    dot_general x4, matrix products, head_terms(): jnp.einsum('gts,tgd->sd', probs, o_blk, preferred_element_type=jnp.float32)  10.5 us
    unnamed x68, local copies, waits for them, and re-layouts  10.3 us
  transfers between devices with their start and end apart: 34, of which 14 were waited for; matrix products, arithmetic and copies ran while one was open for 5% of the time, Pallas kernels for 0%

commit v1 on v0

v1 whole, which is shorter than its diff:
```python
import jax
import jax.numpy as jnp
from jax import lax
from jax.experimental import pallas as pl
from jax.experimental.pallas import tpu as pltpu
from jax.sharding import PartitionSpec as P

MESH = pl.DeviceIdType.MESH
SCALE = 168.0 ** -0.5
LOG2E = 1.4426950408889634
NEG = -1.0e30
T = 128
HALF = 512
WIN = 1536
SPAN = 1152
NZ = 8
F32 = jnp.float32
BF16 = jnp.bfloat16


def dims(lhs, rhs, lc, rc):
    return lax.dot_general(lhs, rhs, (((lc,), (rc,)), ((), ())), preferred_element_type=F32)


def kernel(
    x_ref, q_ref, k_ref, v_ref, o_ref, doc_ref,
    dq_out, dk_out, dv_out, wk_out, wv_out,
    qb, ob, kv, xb, acck, accv, lo_ref, dqs, ts, ps, t2s, tr2, gs, gb, pbuf, sdn, sup, rdn, rup,
    a_send, a_kv, a_q, z_send, z_recv, s_send, s_recv, x_send, x_recv, xs_sem,
    dq_send, dq_recv, t_sem, d_send, d_recv, dn_sem, up_sem,
):
    seq = lax.axis_index("seq")
    head = lax.axis_index("head")
    z = seq // 8
    i = seq % 8
    xl = head // 2
    core = head % 2
    own_half = i // 4
    lane = i % 4
    self_a = core == own_half

    def dev(zz, ii, cc):
        return (zz * 8 + ii, xl * 2 + cc)

    up = lax.rem(z + 1, NZ)
    down = lax.rem(z + NZ - 1, NZ)
    sibling = dev(z, i, 1 - core)
    above = dev(up, i, core)
    below = dev(down, i, core)

    def remote(src, dst, ssem, rsem, device):
        return pltpu.make_async_remote_copy(
            src_ref=src, dst_ref=dst, send_sem=ssem, recv_sem=rsem, device_id=device, device_id_type=MESH)

    def got(dst, sem):
        pltpu.make_async_copy(dst, dst, sem).wait()

    barrier = pltpu.get_barrier_semaphore()

    @pl.loop(1, 8)
    def _(step):
        for cc in range(2):
            pl.semaphore_signal(barrier, inc=1, device_id=dev(z, lax.rem(i + step, 8), cc), device_id_type=MESH)

    for other in (sibling, above, below):
        pl.semaphore_signal(barrier, inc=1, device_id=other, device_id_type=MESH)
    pl.semaphore_wait(barrier, 17)

    def a_parts(l):
        row = pl.multiple_of(lane * T, T)
        c1 = pl.multiple_of(l * T, T)
        c2 = pl.multiple_of(l * 2 * T, 2 * T)
        return (
            (k_ref.at[:, pl.ds(c1, T)], kv.at[pl.ds(1024 + row, T), pl.ds(0, T)], a_send.at[l, 0], a_kv.at[lane, 0]),
            (v_ref.at[:, pl.ds(c1, T)], kv.at[pl.ds(1024 + row, T), pl.ds(T, T)], a_send.at[l, 1], a_kv.at[lane, 1]),
            (q_ref.at[:, pl.ds(c2, 2 * T)], qb.at[pl.ds(row, T)], a_send.at[l, 2], a_q.at[lane, 0]),
            (o_ref.at[:, pl.ds(c2, 2 * T)], ob.at[pl.ds(row, T)], a_send.at[l, 3], a_q.at[lane, 1]),
        )

    def a_start(first, last):
        @pl.loop(0, 4)
        def _(step):
            l = lax.rem(lane + step, 4)
            mine = self_a & (l == lane)

            @pl.when(mine)
            def _():
                for src, dst, ssem, rsem in a_parts(l)[first:last]:
                    pltpu.make_async_copy(src, dst, rsem).start()

            @pl.when(jnp.logical_not(mine))
            def _():
                for src, dst, ssem, rsem in a_parts(l)[first:last]:
                    remote(src, dst, ssem, rsem, dev(z, 4 * core + l, own_half)).start()

    a_start(0, 2)
    a_start(2, 4)

    def x_part(ii):
        start = pl.multiple_of(84 * ii - 4 * (ii % 4), 16)
        zs = pl.ds(4 * core, 4)
        return x_ref.at[zs, pl.ds(start, 96), :], xb.at[zs, :, pl.ds(pl.multiple_of(i * T, T), T)]

    def x_copy(step):
        ii = lax.rem(i + step, 8)
        src, dst = x_part(ii)
        return remote(src, dst, x_send.at[step], x_recv.at[i], dev(z, ii, core))

    src, dst = x_part(i)
    pltpu.make_async_copy(src, dst, x_recv.at[i]).start()

    @pl.loop(1, 8)
    def _(step):
        x_copy(step).start()

    ids = doc_ref[pl.ds((2 * z + core) * 4, 4), :]
    table = doc_ref[...]
    begin = jnp.zeros((4, T), F32)
    for d in range(15):
        count = jnp.sum(jnp.where(table == d, 1.0, 0.0), axis=(0, 1), keepdims=True)
        begin = begin + jnp.where(ids > d, 1.0, 0.0) * count
    begin = begin.astype(jnp.int32) - (2 * z + core - 2) * HALF
    place = lax.broadcasted_iota(jnp.int32, (4, T), 1) + lax.broadcasted_iota(jnp.int32, (4, T), 0) * T
    lo_ref[0:4, :] = jnp.maximum(begin, place + 1)

    acck[...] = jnp.zeros_like(acck)
    accv[...] = jnp.zeros_like(accv)

    def rows(base, m):
        return pl.ds(pl.multiple_of(base + m * T, T), T)

    def z_copy(m):
        return remote(kv.at[rows(1024, m)], kv.at[rows(0, m)], z_send.at[m], z_recv.at[m], above)

    def s_copy(m):
        base = jnp.where(core == 0, 1024, 0)
        return remote(kv.at[rows(base, m)], kv.at[rows(512, m)], s_send.at[m], s_recv.at[m], sibling)

    @pl.loop(0, 4)
    def _(m):
        got(kv.at[rows(1024, m), pl.ds(0, T)], a_kv.at[m, 0])
        got(kv.at[rows(1024, m), pl.ds(T, T)], a_kv.at[m, 1])
        z_copy(m).start()

        @pl.when(core == 0)
        def _():
            s_copy(m).start()

    @pl.loop(0, 4)
    def _(m):
        z_copy(m).wait_recv()

        @pl.when(core == 1)
        def _():
            s_copy(m).start()

    @pl.loop(0, 4)
    def _(m):
        s_copy(m).wait_recv()
        got(qb.at[rows(0, m)], a_q.at[m, 0])
        got(ob.at[rows(0, m)], a_q.at[m, 1])

    @pl.loop(0, 4)
    def _(b):
        here = rows(0, b)
        span = pl.ds(pl.multiple_of(b * T, T), SPAN)
        q2 = jnp.concatenate([qb[here, 0:T], qb[here, T:2 * T]], 0)
        o2 = jnp.concatenate([ob[here, 0:T], ob[here, T:2 * T]], 0)
        kk = kv[span, 0:T]
        vv = kv[span, T:2 * T]
        scores = dims(kk, q2, 1, 1)
        spot = lax.broadcasted_iota(jnp.int32, (SPAN, 2 * T), 0)
        low = lo_ref[pl.ds(b, 1), :] - b * T
        low = jnp.concatenate([low, low], 1)
        high = 1024 + lax.broadcasted_iota(jnp.int32, (1, 2 * T), 1) % T
        scores = jnp.where((spot >= low) & (spot <= high), scores, NEG)
        top = jnp.max(scores, axis=0, keepdims=True)
        expo = jnp.exp2((scores - top) * (SCALE * LOG2E))
        probs = expo * (1.0 / jnp.sum(expo, axis=0, keepdims=True))
        grad_probs = dims(vv, o2, 1, 1)
        delta = jnp.sum(probs * grad_probs, axis=0, keepdims=True)
        grad_scores = (SCALE * probs * (grad_probs - delta)).astype(BF16)
        accv[span, :] += dims(probs.astype(BF16), o2, 1, 0)
        acck[span, :] += dims(grad_scores, q2, 1, 0)
        dq2 = dims(grad_scores, kk, 0, 0).astype(BF16)
        dqs[here, 0:T] = dq2[:T]
        dqs[here, T:2 * T] = dq2[T:]

    def ts_copy():
        return remote(ts, ps, t_sem.at[0], t_sem.at[1], sibling)

    def t2_copy():
        return remote(t2s, tr2, t_sem.at[2], t_sem.at[3], below)

    def put_terms():
        t2s[:, 0:T] = acck[0:512, :].astype(BF16)
        t2s[:, T:2 * T] = accv[0:512, :].astype(BF16)
        t2_copy().start()

    ts[:, 0:T] = acck[512:1024, :].astype(BF16)
    ts[:, T:2 * T] = accv[512:1024, :].astype(BF16)
    ts_copy().start()

    @pl.when(core == 0)
    def _():
        put_terms()

    def dq_copy(m):
        col = pl.ds(pl.multiple_of(lane * 2 * T, 2 * T), 2 * T)
        return dqs.at[rows(0, m)], dq_out.at[:, col], dq_send.at[m], dq_recv.at[lane], dev(z, 4 * core + m, own_half)

    @pl.loop(0, 4)
    def _(m):
        mine = self_a & (m == lane)
        src, dst, ssem, rsem, to = dq_copy(m)

        @pl.when(mine)
        def _():
            pltpu.make_async_copy(src, dst, rsem).start()

        @pl.when(jnp.logical_not(mine))
        def _():
            remote(src, dst, ssem, rsem, to).start()

    ts_copy().wait_recv()
    base = pl.ds(pl.multiple_of(jnp.where(core == 0, 1024, 0), 512), 512)
    acck[base, :] += ps[:, 0:T].astype(F32)
    accv[base, :] += ps[:, T:2 * T].astype(F32)

    @pl.when(core == 1)
    def _():
        put_terms()

    @pl.loop(0, 8)
    def _(j):
        zs = pl.ds(4 * core, 4)
        got(xb.at[zs, :, pl.ds(pl.multiple_of(j * T, T), T)], x_recv.at[j])

    def xs_copy():
        half = xb.at[pl.ds(4 * core, 4)]
        return remote(half, half, xs_sem.at[0], xs_sem.at[1], sibling)

    xs_copy().start()

    t2_copy().wait_recv()
    gs[0] = (accv[1024:1536, :] + tr2[:, T:2 * T].astype(F32)).astype(BF16)
    gs[1] = (acck[1024:1536, :] + tr2[:, 0:T].astype(F32)).astype(BF16)

    def d_copy(part, step):
        ii = lax.rem(i + step, 8)
        dst = gb.at[part, pl.ds(pl.multiple_of(core * HALF, HALF), HALF), pl.ds(pl.multiple_of(lane * T, T), T)]
        return gs.at[part], dst, d_send.at[part, step], d_recv.at[part, lane * 2 + core], dev(z, ii, own_half)

    for part in range(2):
        src, dst, ssem, rsem, to = d_copy(part, 0)

        @pl.when(self_a)
        def _():
            pltpu.make_async_copy(src, dst, rsem).start()

        @pl.when(jnp.logical_not(self_a))
        def _():
            remote(src, dst, ssem, rsem, to).start()

        @pl.loop(1, 8)
        def _(step):
            src, dst, ssem, rsem, to = d_copy(part, step)
            remote(src, dst, ssem, rsem, to).start()

    xs_copy().wait_recv()

    def dest(offset):
        return lax.rem(z + offset + NZ, NZ)

    def long_copy(part, k):
        to = below if part == 0 else above
        return remote(sdn.at[part, k], rdn.at[part, k], dn_sem.at[0, part, k], dn_sem.at[1, part, k], to)

    def short_copy(part, k):
        to = above if part == 0 else below
        return remote(sup.at[part, k], rup.at[part, k], up_sem.at[0, part, k], up_sem.at[1, part, k], to)

    def sign(part):
        return -1 if part == 0 else 1

    def ring(part, k):
        far = dest(sign(part) * (4 - k))
        value = pbuf[part, far]
        if k > 0:
            long_copy(part, k - 1).wait_recv()
            value = value + rdn[part, k - 1].astype(F32)
        sdn[part, k] = value.astype(BF16)
        long_copy(part, k).start()
        if k < 3:
            near = dest(-sign(part) * (3 - k))
            value = pbuf[part, near]
            if k > 0:
                short_copy(part, k - 1).wait_recv()
                value = value + rup[part, k - 1].astype(F32)
            sup[part, k] = value.astype(BF16)
            short_copy(part, k).start()

    for part in range(2):
        @pl.loop(0, 8)
        def _(n):
            dst = gb.at[part, pl.ds(pl.multiple_of((n % 2) * HALF, HALF), HALF),
                        pl.ds(pl.multiple_of((n // 2) * T, T), T)]
            got(dst, d_recv.at[part, n])

        @pl.loop(0, 4)
        def _(n):
            lhs = xb[pl.ds(2 * n, 2)].reshape(192, 1024)
            pbuf[part, pl.ds(2 * n, 2)] = jnp.dot(lhs, gb[part], preferred_element_type=F32).reshape(2, 96, 512)

        ring(part, 0)

    mine = pl.ds(pl.multiple_of(i * T, T), T)
    dv_out[...] = gb[0, mine, :]
    dk_out[...] = gb[1, mine, :]

    for k in range(1, 4):
        for part in range(2):
            ring(part, k)

    offset = 4 * (i % 4)
    for part in range(2):
        long_copy(part, 3).wait_recv()
        short_copy(part, 2).wait_recv()
        total = pbuf[part, z] + rdn[part, 3].astype(F32) + rup[part, 2].astype(F32)
        out = wv_out if part == 0 else wk_out
        out[...] = pltpu.roll(total, lax.rem(96 - offset, 96), 0)[:84]

    @pl.loop(0, 4)
    def _(l):
        got(dq_out.at[:, pl.ds(pl.multiple_of(l * 2 * T, 2 * T), 2 * T)], dq_recv.at[l])

    @pl.loop(0, 4)
    def _(m):
        z_copy(m).wait_send()
        s_copy(m).wait_send()
        src, dst, ssem, rsem, to = dq_copy(m)

        @pl.when(jnp.logical_not(self_a & (m == lane)))
        def _():
            for src_a, dst_a, ssem_a, rsem_a in a_parts(m):
                remote(src_a, dst_a, ssem_a, rsem_a, dev(z, 4 * core + m, own_half)).wait_send()
            remote(src, dst, ssem, rsem, to).wait_send()

    ts_copy().wait_send()
    t2_copy().wait_send()
    xs_copy().wait_send()

    @pl.loop(1, 8)
    def _(step):
        x_copy(step).wait_send()

    for part in range(2):
        src, dst, ssem, rsem, to = d_copy(part, 0)

        @pl.when(jnp.logical_not(self_a))
        def _():
            remote(src, dst, ssem, rsem, to).wait_send()

        @pl.loop(1, 8)
        def _(step):
            src, dst, ssem, rsem, to = d_copy(part, step)
            remote(src, dst, ssem, rsem, to).wait_send()

        for k in range(4):
            long_copy(part, k).wait_send()
        for k in range(3):
            short_copy(part, k).wait_send()


def local(inputs, queries, keys, values, grad_out, doc_ids):
    x = inputs.reshape(8, 672, 128)
    docs = doc_ids.reshape(64, 128)
    any_space = pl.BlockSpec(memory_space=pl.ANY)
    vmem = pl.BlockSpec(memory_space=pltpu.VMEM)
    dma = pltpu.SemaphoreType.DMA
    shape = jax.ShapeDtypeStruct
    return tuple(pl.pallas_call(
        kernel,
        name="window_backward",
        out_shape=(
            shape((T, 1024), BF16), shape((T, 512), BF16), shape((T, 512), BF16),
            shape((84, 512), F32), shape((84, 512), F32)),
        in_specs=[any_space] * 5 + [vmem],
        out_specs=(vmem,) * 5,
        scratch_shapes=[
            pltpu.VMEM((512, 256), BF16), pltpu.VMEM((512, 256), BF16), pltpu.VMEM((WIN, 256), BF16),
            pltpu.VMEM((8, 96, 1024), BF16), pltpu.VMEM((WIN, T), F32), pltpu.VMEM((WIN, T), F32),
            pltpu.VMEM((8, T), jnp.int32), pltpu.VMEM((512, 256), BF16),
            pltpu.VMEM((512, 256), BF16), pltpu.VMEM((512, 256), BF16), pltpu.VMEM((512, 256), BF16),
            pltpu.VMEM((512, 256), BF16), pltpu.VMEM((2, 512, T), BF16), pltpu.VMEM((2, 1024, 512), BF16),
            pltpu.VMEM((2, 8, 96, 512), F32),
            pltpu.VMEM((2, 4, 96, 512), BF16), pltpu.VMEM((2, 3, 96, 512), BF16),
            pltpu.VMEM((2, 4, 96, 512), BF16), pltpu.VMEM((2, 3, 96, 512), BF16),
            dma((4, 4)), dma((4, 2)), dma((4, 2)), dma((4,)), dma((4,)), dma((4,)), dma((4,)), dma((8,)), dma((8,)),
            dma((2,)), dma((4,)), dma((4,)), dma((4,)), dma((2, 8)), dma((2, 8)), dma((2, 2, 4)), dma((2, 2, 3)),
        ],
        compiler_params=pltpu.CompilerParams(
            collective_id=0, has_side_effects=True, vmem_limit_bytes=48 << 20),
        cost_estimate=pl.CostEstimate(flops=3_000_000_000, bytes_accessed=12_000_000, transcendentals=1_200_000),
    )(x, queries, keys, values, grad_out, docs))


def solution(mesh):
    return jax.shard_map(
        local,
        mesh=mesh,
        in_specs=(P(None, "seq"), P("seq", "head"), P("seq", "head"), P("seq", "head"), P("seq", "head"), P()),
        out_specs=(P("seq", "head"),) * 5,
        check_vma=False,
    )
```

time: 485 us -> 96.1 us (0.20)
  waiting for transfers between devices: 269 us -> 0 us
  starting transfers between devices: 130 us -> 0 us
  Pallas kernels: 0 us -> 86 us
  matrix products: 42.9 us -> 0 us
  between operations: 15 us -> 0.66 us
  local copies, waits for them, and re-layouts: 18 us -> 9.15 us
  other arithmetic: 4.99 us -> 0 us
    all_gather x1 -> x0, waiting for transfers between devices: 225 us -> none  [local(): every = lax.all_gather(both, 'seq', axis=0, tiled=True)]
    ppermute x32 -> x0, starting transfers between devices: 98.8 us -> none  [passed_along(): lax.ppermute(value, axis, [(source, source + steps) for source in range(i...]
    pallas_call x0 -> x1, Pallas kernels: none -> 86 us  [local(): pl.pallas_call(kernel, name='window_backward', out_shape=(shape((T, 1024)...]
    dot_general x17 -> x0, matrix products: 35.5 us -> none  [the longest x1 11 us: local(): summed = jnp.dot(features, every, preferred_element_type=jnp.float32)]
    all_to_all x1 -> x0, starting transfers between devices: 31.3 us -> none  [local(): lax.all_to_all(inputs, 'seq', split_axis=0, concat_axis=1, tiled=True)]
    ppermute x32 -> x0, waiting for transfers between devices: 31.3 us -> none  [passed_along(): lax.ppermute(value, axis, [(source, source + steps) for source in range(i...]
    all_to_all x1 -> x0, waiting for transfers between devices: 13.1 us -> none  [local(): lax.all_to_all(inputs, 'seq', split_axis=0, concat_axis=1, tiled=True)]
    sub x4 -> x0, matrix products: 7.32 us -> none  [head_terms(): expo = jnp.exp(scores - top)]
  transfers between devices with their start and end apart: 34 -> 0, of which waited for: 14 -> 0; matrix products, arithmetic and copies ran while one was open for 5% -> 0% of each run, Pallas kernels for 0% -> 0%
where the time goes in v1:
time: 96.1 us; the launch traced here: 95.8 us
  Pallas kernels  86 us (89%)
  local copies, waits for them, and re-layouts  9.15 us (10%)
    pallas_call x1, Pallas kernels, local(): pl.pallas_call(kernel, name='window_backward', out_shape=(shape((T, 1024)...  86 us
    unnamed x17, local copies, waits for them, and re-layouts  9.15 us

profile of v1, /device:TPU:4, one launch (start us, length us, event | category | flops | bytes accessed | tf_op | source)
XLA Modules:
  0.0 95.8 jit_solution(3439580425237773146)
XLA Ops:
  0.6 0.0 copy-start
  0.6 1.3 %copy-done = bf16[5376,128]{1,0:T(8,128)(2,1)S(1)} copy-done((bf16[5376,128]{1,0:T(8,128)(2,1)S(1)}, bf16[5376,128]{1,0:T(8,128)(2,1)}, u32[]{:S(2)}) %copy-start) | copy-done | bytes 1376280
  2.0 0.0 copy-start.1
  2.0 0.9 copy-done.1
  2.9 0.0 copy-start.2
  2.9 0.9 copy-done.2
  3.9 0.0 copy-start.3
  3.9 0.9 copy-done.3
  4.8 0.0 copy-start.4
  4.8 0.9 copy-done.4
  5.7 0.0 copy-start.5
  5.7 0.8 copy-done.5
  6.4 86.0 %window_backward.1 = (bf16[128,1024]{1,0:T(8,128)(2,1)S(1)}, bf16[128,512]{1,0:T(8,128)(2,1)S(1)}, bf16[128,512]{1,0:T(8,128)(2,1)S(1)}, f32[84,512]{1,0:T(8,128)S(1)}, f32[84,512]{1,0:T(8,128)S(1)}) custom-call(bf16[8,672,128]{2,1,0:T(8,128)(2,1)S(1)} %bitcast.2, bf16[128,1024]{1,0:T(8,128)(2,1)S(1)} %copy-done.1, bf16[128,512]{1,0:T(8,128)(2,1)S(1)} %copy-done.3, ...), custom_call_target="tpu_custom_call" | custom-call | flops 3000000000 | bytes 12000000 | tf_op jit(solution)/shard_map/window_backward/pallas_call | solution.py:382
  92.4 0.7 copy.16
  93.1 0.7 copy.17
  93.8 0.7 copy.18
  94.5 0.7 copy.19
  95.1 0.7 copy.20
Async XLA Ops:
  0.6 1.3 %copy-start = (bf16[5376,128]{1,0:T(8,128)(2,1)S(1)}, bf16[5376,128]{1,0:T(8,128)(2,1)}, u32[]{:S(2)}) copy-start(bf16[5376,128]{1,0:T(8,128)(2,1)} %param.6) | copy-start | bytes 4128772
  2.0 0.9 copy-start.1
  2.9 0.9 copy-start.2
  3.9 0.9 copy-start.3
  4.8 0.9 copy-start.4
  5.7 0.8 copy-start.5

commit v2 on v1

v2 whole, which is shorter than its diff:
```python
import jax
import jax.numpy as jnp
from jax import lax
from jax.experimental import pallas as pl
from jax.experimental.pallas import tpu as pltpu
from jax.sharding import PartitionSpec as P

MESH = pl.DeviceIdType.MESH
SCALE = 168.0 ** -0.5
LOG2E = 1.4426950408889634
NEG = -1.0e30
T = 128
HALF = 512
WIN = 1536
SPAN = 1152
NZ = 8
F32 = jnp.float32
BF16 = jnp.bfloat16


def dims(lhs, rhs, lc, rc):
    return lax.dot_general(lhs, rhs, (((lc,), (rc,)), ((), ())), preferred_element_type=F32)


def kernel(
    x_ref, q_ref, k_ref, v_ref, o_ref, doc_hbm,
    dq_out, dk_out, dv_out, wk_out, wv_out,
    qb, ob, kv, xb, acck, accv, lo_ref, dqs, t1s, tr1, t2s, tr2, gs, gb, pbuf, sdn, sup, rdn, rup, doc_ref, fin, precv,
    a_send, a_kv, a_q, z_send, z_recv, s_send, s_recv, x_send, x_recv, xs_sem,
    dq_send, dq_recv, t1_sem, t2_sem, d_send, d_recv, f_send, dn_send, dn_recv, up_send, up_recv, doc_sem, out_sem, g_send, g_recv, p_sem,
    xf_send, xf_recv,
):
    seq = lax.axis_index("seq")
    head = lax.axis_index("head")
    z = seq // 8
    i = seq % 8
    xl = head // 2
    core = head % 2
    own_half = i // 4
    lane = i % 4
    self_a = core == own_half
    y = i // 2
    xh = i % 2

    def dev(zz, ii, cc):
        return (zz * 8 + ii, xl * 2 + cc)

    up = lax.rem(z + 1, NZ)
    down = lax.rem(z + NZ - 1, NZ)
    sibling = dev(z, i, 1 - core)
    above = dev(up, i, core)
    below = dev(down, i, core)

    def remote(src, dst, ssem, rsem, device):
        return pltpu.make_async_remote_copy(
            src_ref=src, dst_ref=dst, send_sem=ssem, recv_sem=rsem, device_id=device, device_id_type=MESH)

    def got(dst, sem):
        pltpu.make_async_copy(dst, dst, sem).wait()

    docs = pltpu.make_async_copy(doc_hbm, doc_ref, doc_sem)
    docs.start()
    barrier = pltpu.get_barrier_semaphore()

    @pl.loop(1, 8)
    def _(step):
        for cc in range(2):
            pl.semaphore_signal(barrier, inc=1, device_id=dev(z, lax.rem(i + step, 8), cc), device_id_type=MESH)

    across = dev(jnp.where(core == 0, down, up), i, 1 - core)
    flip = i + 1 - 2 * xh
    opposite = (z * 8 + flip, (1 - xl) * 2 + core)
    for other in (sibling, above, below, across, opposite, dev(up, flip, core), dev(down, flip, core)):
        pl.semaphore_signal(barrier, inc=1, device_id=other, device_id_type=MESH)
    pl.semaphore_wait(barrier, 21)

    def a_parts(l):
        row = pl.multiple_of(lane * T, T)
        c1 = pl.multiple_of(l * T, T)
        c2 = pl.multiple_of(l * 2 * T, 2 * T)
        return (
            (k_ref.at[:, pl.ds(c1, T)], kv.at[pl.ds(1024 + row, T), pl.ds(0, T)], a_send.at[l, 0], a_kv.at[lane, 0]),
            (v_ref.at[:, pl.ds(c1, T)], kv.at[pl.ds(1024 + row, T), pl.ds(T, T)], a_send.at[l, 1], a_kv.at[lane, 1]),
            (q_ref.at[:, pl.ds(c2, 2 * T)], qb.at[pl.ds(row, T)], a_send.at[l, 2], a_q.at[lane, 0]),
            (o_ref.at[:, pl.ds(c2, 2 * T)], ob.at[pl.ds(row, T)], a_send.at[l, 3], a_q.at[lane, 1]),
        )

    def a_start(first, last):
        @pl.loop(0, 4)
        def _(step):
            l = lax.rem(lane + step, 4)
            mine = self_a & (l == lane)

            @pl.when(mine)
            def _():
                for src, dst, ssem, rsem in a_parts(l)[first:last]:
                    pltpu.make_async_copy(src, dst, rsem).start()

            @pl.when(jnp.logical_not(mine))
            def _():
                for src, dst, ssem, rsem in a_parts(l)[first:last]:
                    remote(src, dst, ssem, rsem, dev(z, 4 * core + l, own_half)).start()

    a_start(0, 2)
    a_start(2, 4)

    def x_part(yy, sub):
        row = 2 * yy + sub
        start = pl.multiple_of(84 * row - 4 * (row % 4), 16)
        zs = pl.ds(4 * core, 4)
        return x_ref.at[zs, pl.ds(start, 96), :], xb.at[sub, zs, :, pl.ds(pl.multiple_of(i * T, T), T)]

    def x_copy(step, sub):
        yy = lax.rem(y + step, 4)
        src, dst = x_part(yy, sub)
        return remote(src, dst, x_send.at[step, sub], x_recv.at[y, sub], dev(z, yy * 2 + xh, core))

    def x_start():
        for sub in range(2):
            src, dst = x_part(y, sub)
            pltpu.make_async_copy(src, dst, x_recv.at[y, sub]).start()

        @pl.loop(1, 4)
        def _(step):
            for sub in range(2):
                x_copy(step, sub).start()

    def x_tokens(j):
        return pl.ds(pl.multiple_of(j * T, T), T)

    def x_across(ys):
        piece = xb.at[:, pl.ds(4 * core, 4), :, x_tokens(ys * 2 + xh)]
        return remote(piece, piece, xf_send.at[ys], xf_recv.at[ys], opposite)

    def x_forward(step):
        ys = lax.rem(y + step, 4)
        for sub in range(2):
            got(xb.at[sub, pl.ds(4 * core, 4), :, x_tokens(ys * 2 + xh)], x_recv.at[ys, sub])
        x_across(ys).start()

    docs.wait()
    ids = doc_ref[pl.ds((2 * z + core) * 4, 4), :]
    table = doc_ref[...]
    begin = jnp.zeros((4, T), F32)
    for d in range(15):
        count = jnp.sum(jnp.where(table == d, 1.0, 0.0), axis=(0, 1), keepdims=True)
        begin = begin + jnp.where(ids > d, 1.0, 0.0) * count
    begin = begin.astype(jnp.int32) - (2 * z + core - 2) * HALF
    place = lax.broadcasted_iota(jnp.int32, (4, T), 1) + lax.broadcasted_iota(jnp.int32, (4, T), 0) * T
    lo_ref[0:4, :] = jnp.maximum(begin, place + 1)

    acck[...] = jnp.zeros_like(acck)
    accv[...] = jnp.zeros_like(accv)

    def rows(base, m):
        return pl.ds(pl.multiple_of(base + m * T, T), T)

    def z_copy(m):
        return remote(kv.at[rows(1024, m)], kv.at[rows(0, m)], z_send.at[m], z_recv.at[m], above)

    def s_copy(m):
        base = jnp.where(core == 0, 1024, 0)
        return remote(kv.at[rows(base, m)], kv.at[rows(512, m)], s_send.at[m], s_recv.at[m], sibling)

    @pl.loop(0, 4)
    def _(m):
        got(kv.at[rows(1024, m), pl.ds(0, T)], a_kv.at[m, 0])
        got(kv.at[rows(1024, m), pl.ds(T, T)], a_kv.at[m, 1])
        z_copy(m).start()

        @pl.when(core == 0)
        def _():
            s_copy(m).start()

    x_start()

    @pl.loop(0, 4)
    def _(m):
        z_copy(m).wait_recv()

        @pl.when(core == 1)
        def _():
            s_copy(m).start()

    @pl.loop(0, 4)
    def _(m):
        s_copy(m).wait_recv()
        got(qb.at[rows(0, m)], a_q.at[m, 0])
        got(ob.at[rows(0, m)], a_q.at[m, 1])

    def t2_copy(b):
        return remote(t2s.at[rows(0, b)], tr2.at[rows(0, b)], t2_sem.at[0, b], t2_sem.at[1, b], below)

    def dq_copy(m):
        col = pl.ds(pl.multiple_of(lane * 2 * T, 2 * T), 2 * T)
        return dqs.at[rows(0, m)], dq_out.at[:, col], dq_send.at[m], dq_recv.at[lane], dev(z, 4 * core + m, own_half)

    @pl.loop(0, 4)
    def _(b):
        here = rows(0, b)
        span = pl.ds(pl.multiple_of(b * T, T), SPAN)
        q2 = jnp.concatenate([qb[here, 0:T], qb[here, T:2 * T]], 0)
        o2 = jnp.concatenate([ob[here, 0:T], ob[here, T:2 * T]], 0)
        kk = kv[span, 0:T]
        vv = kv[span, T:2 * T]
        scores = dims(kk, q2, 1, 1)
        x_forward(b)
        spot = lax.broadcasted_iota(jnp.int32, (SPAN, 2 * T), 0)
        low = lo_ref[pl.ds(b, 1), :] - b * T
        low = jnp.concatenate([low, low], 1)
        high = 1024 + lax.broadcasted_iota(jnp.int32, (1, 2 * T), 1) % T
        scores = jnp.where((spot >= low) & (spot <= high), scores, NEG)
        top = jnp.max(scores, axis=0, keepdims=True)
        expo = jnp.exp2((scores - top) * (SCALE * LOG2E))
        probs = expo * (1.0 / jnp.sum(expo, axis=0, keepdims=True))
        grad_probs = dims(vv, o2, 1, 1)
        delta = jnp.sum(probs * grad_probs, axis=0, keepdims=True)
        grad_scores = (SCALE * probs * (grad_probs - delta)).astype(BF16)
        accv[span, :] += dims(probs.astype(BF16), o2, 1, 0)
        acck[span, :] += dims(grad_scores, q2, 1, 0)
        t2s[here, 0:T] = acck[here, :].astype(BF16)
        t2s[here, T:2 * T] = accv[here, :].astype(BF16)
        t2_copy(b).start()
        dq2 = dims(grad_scores, kk, 0, 0).astype(BF16)
        dqs[here, 0:T] = dq2[:T]
        dqs[here, T:2 * T] = dq2[T:]
        mine = self_a & (b == lane)
        src, dst, ssem, rsem, to = dq_copy(b)

        @pl.when(mine)
        def _():
            pltpu.make_async_copy(src, dst, rsem).start()

        @pl.when(jnp.logical_not(mine))
        def _():
            remote(src, dst, ssem, rsem, to).start()

    owner = dev(jnp.where(core == 0, down, z), i, 1 - core)

    def t1_copy(part):
        return remote(t1s.at[part], tr1.at[part], t1_sem.at[0, part], t1_sem.at[1, part], owner)

    for part, total in enumerate((accv, acck)):
        t1s[part] = total[512:1024, :].astype(BF16)
        t1_copy(part).start()

    @pl.loop(0, 4)
    def _(b):
        t2_copy(b).wait_recv()

    right = lax.rem(y + 1, 4) * 2 + xh
    left = lax.rem(y + 3, 4) * 2 + xh

    def block(part, u, a, h):
        return gb.at[part, pl.ds(pl.multiple_of(a * HALF + h * 256, 256), 256), pl.ds(pl.multiple_of(u * T, T), T)]

    def d_copy(part, n, h):
        to = dev(z, (right, left, i)[n], own_half)
        return (gs.at[part, pl.ds(h * 256, 256)], block(part, y % 2, core, h), d_send.at[part, n, h],
                d_recv.at[part, (y % 2) * 4 + core * 2 + h], to)

    def forward(part, u, a, h):
        piece = block(part, u, a, h)
        n = u * 4 + a * 2 + h
        return remote(piece, piece, f_send.at[part, n], d_recv.at[part, n], dev(z, jnp.where(h == 0, right, left), core))

    def arrived(part, u, a, h):
        got(block(part, u, a, h), d_recv.at[part, u * 4 + a * 2 + h])

    def steps_from(u):
        return lax.rem(y - 2 * core - u + 8, 4)

    def first_send(part):
        for h in range(2):
            for n in range(2):
                src, dst, ssem, rsem, to = d_copy(part, n, (h + n) % 2)
                remote(src, dst, ssem, rsem, to).start()
        for h in range(2):
            src, dst, ssem, rsem, to = d_copy(part, 2, h)

            @pl.when(self_a)
            def _():
                pltpu.make_async_copy(src, dst, rsem).start()

            @pl.when(jnp.logical_not(self_a))
            def _():
                remote(src, dst, ssem, rsem, to).start()

    def forward_side(part):
        @pl.loop(0, 4)
        def _(e):
            u, a = e // 2, e % 2
            steps = steps_from(u)

            @pl.when((steps == 1) | (steps == 3))
            def _():
                h = jnp.where(steps == 1, 0, 1)
                arrived(part, u, a, h)
                forward(part, u, a, h).start()

    def gathered(part):
        @pl.loop(0, 4)
        def _(e):
            u, a = e // 2, e % 2
            steps = steps_from(u)

            @pl.when((steps == 2) | (steps == 0))
            def _():
                arrived(part, u, a, 0)
                arrived(part, u, a, 1)

            @pl.when((steps == 1) | (steps == 3))
            def _():
                arrived(part, u, a, jnp.where(steps == 1, 1, 0))

    def sent(part):
        for n in range(2):
            for h in range(2):
                src, dst, ssem, rsem, to = d_copy(part, n, h)
                remote(src, dst, ssem, rsem, to).wait_send()

        @pl.when(jnp.logical_not(self_a))
        def _():
            for h in range(2):
                src, dst, ssem, rsem, to = d_copy(part, 2, h)
                remote(src, dst, ssem, rsem, to).wait_send()

        @pl.loop(0, 4)
        def _(e):
            u, a = e // 2, e % 2
            steps = steps_from(u)

            @pl.when((steps == 1) | (steps == 3))
            def _():
                forward(part, u, a, jnp.where(steps == 1, 0, 1)).wait_send()

    def g_copy(part, m):
        col = pl.ds(pl.multiple_of(lane * T, T), T)
        return (gs.at[part, rows(0, m)], (dv_out, dk_out)[part].at[:, col], g_send.at[part, m], g_recv.at[part, lane],
                dev(z, 4 * core + m, own_half))

    def token_send(part):
        @pl.loop(0, 4)
        def _(m):
            mine = self_a & (m == lane)
            src, dst, ssem, rsem, to = g_copy(part, m)

            @pl.when(mine)
            def _():
                pltpu.make_async_copy(src, dst, rsem).start()

            @pl.when(jnp.logical_not(mine))
            def _():
                remote(src, dst, ssem, rsem, to).start()

    def token_wait(part):
        @pl.loop(0, 4)
        def _(m):
            got((dv_out, dk_out)[part].at[:, pl.ds(pl.multiple_of(m * T, T), T)], g_recv.at[part, m])
            src, dst, ssem, rsem, to = g_copy(part, m)

            @pl.when(jnp.logical_not(self_a & (m == lane)))
            def _():
                remote(src, dst, ssem, rsem, to).wait_send()

    for part, total in enumerate((accv, acck)):
        t1_copy(part).wait_recv()
        cols = pl.ds((1 - part) * T, T)
        gs[part] = (total[1024:1536, :] + tr1[part].astype(F32) + tr2[:, cols].astype(F32)).astype(BF16)
        first_send(part)

    @pl.loop(0, 4)
    def _(ys):
        got(xb.at[:, pl.ds(4 * core, 4), :, x_tokens(ys * 2 + 1 - xh)], xf_recv.at[ys])

    def xs_copy():
        half = xb.at[:, pl.ds(4 * core, 4)]
        return remote(half, half, xs_sem.at[0], xs_sem.at[1], sibling)

    xs_copy().start()

    def dest(offset):
        return lax.rem(z + offset + NZ, NZ)

    def long_copy(part, sub, h, k):
        slot, ii = (xh, (i // 2) * 2 + sub) if k == 3 else (sub, i)
        return remote(sdn.at[part, sub, h, k], rdn.at[part, slot, h, k], dn_send.at[part, sub, h, k],
                      dn_recv.at[part, slot, h, k], dev(down if sub == 0 else up, ii, core))

    def short_copy(part, sub, h, k):
        slot, ii = (xh, (i // 2) * 2 + sub) if k == 2 else (sub, i)
        return remote(sup.at[part, sub, h, k], rup.at[part, slot, h, k], up_send.at[part, sub, h, k],
                      up_recv.at[part, slot, h, k], dev(up if sub == 0 else down, ii, core))

    def ring(part, k):
        for h in range(2):
            lines = slice(h * 48, h * 48 + 48)
            for sub in range(2):
                way = -1 if sub == 0 else 1
                value = pbuf[part, sub, dest(way * (4 - k)), lines]
                if k > 0:
                    got(rdn.at[part, sub, h, k - 1], dn_recv.at[part, sub, h, k - 1])
                    value = value + rdn[part, sub, h, k - 1].astype(F32)
                sdn[part, sub, h, k] = value.astype(BF16)
                long_copy(part, sub, h, k).start()
            if k < 3:
                for sub in range(2):
                    way = -1 if sub == 0 else 1
                    value = pbuf[part, sub, dest(-way * (3 - k)), lines]
                    if k > 0:
                        got(rup.at[part, sub, h, k - 1], up_recv.at[part, sub, h, k - 1])
                        value = value + rup[part, sub, h, k - 1].astype(F32)
                    sup[part, sub, h, k] = value.astype(BF16)
                    short_copy(part, sub, h, k).start()

    def product(part):
        @pl.loop(0, 4)
        def _(n):
            at = pl.ds((n % 2) * 4, 4)
            lhs = xb[n // 2, at].reshape(384, 1024)
            pbuf[part, n // 2, at] = jnp.dot(lhs, gb[part], preferred_element_type=F32).reshape(4, 96, 256)

    def p_copy(part):
        return remote(pbuf.at[part, 1 - xh, z], precv.at[part], p_sem.at[0, part], p_sem.at[1, part], dev(z, flip, core))

    offset = 4 * (i % 4)

    def weight_copy(part):
        return pltpu.make_async_copy(fin.at[part], (wv_out, wk_out)[part], out_sem.at[part])

    def finish(part):
        p_copy(part).wait_recv()
        for s in range(2):
            pieces = []
            for h in range(2):
                got(rdn.at[part, s, h, 3], dn_recv.at[part, s, h, 3])
                got(rup.at[part, s, h, 2], up_recv.at[part, s, h, 2])
                pieces.append(rdn[part, s, h, 3].astype(F32) + rup[part, s, h, 2].astype(F32))
            total = jnp.concatenate(pieces, 0) + jnp.where(xh == s, pbuf[part, s, z], precv[part])
            total = pltpu.roll(total, lax.rem(96 - offset, 96), 0)
            for u in range(2):
                fin[part, :, (u * 2 + s) * T:(u * 2 + s + 1) * T] = total[:84, u * T:(u + 1) * T]
        weight_copy(part).start()

    forward_side(0)
    forward_side(1)
    token_send(0)
    token_send(1)
    gathered(0)
    xs_copy().wait_recv()
    product(0)
    ring(0, 0)
    p_copy(0).start()
    ring(0, 1)
    gathered(1)
    product(1)
    ring(1, 0)
    p_copy(1).start()
    ring(0, 2)
    ring(1, 1)
    ring(0, 3)
    ring(1, 2)
    ring(1, 3)
    finish(0)
    finish(1)
    token_wait(0)
    token_wait(1)

    @pl.loop(0, 4)
    def _(l):
        got(dq_out.at[:, pl.ds(pl.multiple_of(l * 2 * T, 2 * T), 2 * T)], dq_recv.at[l])

    @pl.loop(0, 4)
    def _(m):
        z_copy(m).wait_send()
        s_copy(m).wait_send()
        src, dst, ssem, rsem, to = dq_copy(m)

        @pl.when(jnp.logical_not(self_a & (m == lane)))
        def _():
            for src_a, dst_a, ssem_a, rsem_a in a_parts(m):
                remote(src_a, dst_a, ssem_a, rsem_a, dev(z, 4 * core + m, own_half)).wait_send()
            remote(src, dst, ssem, rsem, to).wait_send()

    @pl.loop(0, 4)
    def _(b):
        t2_copy(b).wait_send()

    xs_copy().wait_send()

    @pl.loop(0, 4)
    def _(ys):
        x_across(ys).wait_send()

    @pl.loop(1, 4)
    def _(step):
        for sub in range(2):
            x_copy(step, sub).wait_send()

    for part in range(2):
        t1_copy(part).wait_send()
        sent(part)
        weight_copy(part).wait()
        p_copy(part).wait_send()
        for sub in range(2):
            for h in range(2):
                for k in range(4):
                    long_copy(part, sub, h, k).wait_send()
                for k in range(3):
                    short_copy(part, sub, h, k).wait_send()


def copies(*refs):
    count = 5
    inputs, outputs, held, sem = refs[:count], refs[count:2 * count], refs[2 * count:3 * count], refs[-1]
    loads = [pltpu.make_async_copy(inputs[n], held[n], sem.at[0, n]) for n in range(count)]
    stores = [pltpu.make_async_copy(held[n], outputs[n], sem.at[1, n]) for n in range(count)]
    for load in loads:
        load.start()
    for load, store in zip(loads, stores):
        load.wait()
        store.start()
    for store in stores:
        store.wait()


def local(inputs, queries, keys, values, grad_out, doc_ids):
    x = inputs.reshape(8, 672, 128)
    docs = doc_ids.reshape(64, 128)
    anywhere = pl.BlockSpec(memory_space=pl.ANY)
    dma = pltpu.SemaphoreType.DMA
    shape = jax.ShapeDtypeStruct
    vmem = pltpu.VMEM
    outs = (
        shape((T, 1024), BF16), shape((T, 512), BF16), shape((T, 512), BF16), shape((84, 512), F32), shape((84, 512), F32))
    results = pl.pallas_call(
        kernel,
        name="window_backward",
        out_shape=outs,
        in_specs=[anywhere] * 6,
        out_specs=(anywhere,) * 5,
        scratch_shapes=[
            vmem((512, 256), BF16), vmem((512, 256), BF16), vmem((WIN, 256), BF16),
            vmem((2, 8, 96, 1024), BF16), vmem((WIN, T), F32), vmem((WIN, T), F32),
            vmem((8, T), jnp.int32), vmem((512, 256), BF16),
            vmem((2, 512, T), BF16), vmem((2, 512, T), BF16), vmem((512, 256), BF16), vmem((512, 256), BF16),
            vmem((2, 512, T), BF16), vmem((2, 1024, 256), BF16),
            vmem((2, 2, 8, 96, 256), F32),
            vmem((2, 2, 2, 4, 48, 256), BF16), vmem((2, 2, 2, 3, 48, 256), BF16),
            vmem((2, 2, 2, 4, 48, 256), BF16), vmem((2, 2, 2, 3, 48, 256), BF16), vmem((64, 128), jnp.int32), vmem((2, 84, 512), F32),
            vmem((2, 96, 256), F32),
            dma((4, 4)), dma((4, 2)), dma((4, 2)), dma((4,)), dma((4,)), dma((4,)), dma((4,)), dma((4, 2)), dma((4, 2)), dma((2,)),
            dma((4,)), dma((4,)), dma((2, 2)), dma((2, 4)), dma((2, 3, 2)), dma((2, 8)), dma((2, 8)),
            dma((2, 2, 2, 4)), dma((2, 2, 2, 4)), dma((2, 2, 2, 3)), dma((2, 2, 2, 3)), dma(()), dma((2,)), dma((2, 4)), dma((2, 4)),
            dma((2, 2)), dma((4,)), dma((4,)),
        ],
        compiler_params=pltpu.CompilerParams(
            collective_id=0, has_side_effects=True, vmem_limit_bytes=60 << 20),
        cost_estimate=pl.CostEstimate(flops=3_000_000_000, bytes_accessed=12_000_000, transcendentals=1_200_000),
    )(x, queries, keys, values, grad_out, docs)
    return tuple(pl.pallas_call(
        copies,
        name="results",
        out_shape=outs,
        in_specs=[anywhere] * 5,
        out_specs=(anywhere,) * 5,
        scratch_shapes=[vmem(o.shape, o.dtype) for o in outs] + [dma((2, 5))],
        compiler_params=pltpu.CompilerParams(vmem_limit_bytes=60 << 20),
    )(*results))


def solution(mesh):
    return jax.shard_map(
        local,
        mesh=mesh,
        in_specs=(P(None, "seq"), P("seq", "head"), P("seq", "head"), P("seq", "head"), P("seq", "head"), P()),
        out_specs=(P("seq", "head"),) * 5,
        check_vma=False,
    )
```

time: 96.1 us -> 80.1 us (0.83)
  the two profiles are of different devices: /device:TPU:4 before, /device:TPU:20 now
where the time goes in v2:
time: 80.1 us; the launch traced here: 79.9 us
  Pallas kernels  79.3 us (99%)
    pallas_call x1, Pallas kernels, local(): pl.pallas_call(kernel, name='window_backward', out_shape=outs, in_specs=[...  77.3 us
    pallas_call x1, Pallas kernels, local(): pl.pallas_call(copies, name='results', out_shape=outs, in_specs=[anywhere...  1.95 us

profile of v2, /device:TPU:20, one launch (start us, length us, event | category | flops | bytes accessed | tf_op | source)
XLA Modules:
  0.0 79.9 jit_solution(174309440175872178)
XLA Ops:
  0.6 77.3 %window_backward.1 = (bf16[128,1024]{1,0:T(8,128)(2,1)}, bf16[128,512]{1,0:T(8,128)(2,1)}, bf16[128,512]{1,0:T(8,128)(2,1)}, f32[84,512]{1,0:T(8,128)}, f32[84,512]{1,0:T(8,128)}) custom-call(bf16[8,672,128]{2,1,0:T(8,128)(2,1)} %bitcast.2, bf16[128,1024]{1,0:T(8,128)(2,1)} %q_ref.1, bf16[128,512]{1,0:T(8,128)(2,1)} %k_ref.1, bf16[128,512]{1,0:T(8,128)(2,1)} %v_ref.1, ...), custom_call_target="tpu_custom_call" | custom-call | flops 3000000000 | bytes 12000000 | tf_op jit(solution)/shard_map/window_backward/pallas_call | solution.py:536
  78.0 1.9 %results.1 = (bf16[128,1024]{1,0:T(8,128)(2,1)}, bf16[128,512]{1,0:T(8,128)(2,1)}, bf16[128,512]{1,0:T(8,128)(2,1)}, f32[84,512]{1,0:T(8,128)}, f32[84,512]{1,0:T(8,128)}) custom-call(bf16[128,1024]{1,0:T(8,128)(2,1)} %get-tuple-element.10.refs_0_, bf16[128,512]{1,0:T(8,128)(2,1)} %get-tuple-element.11.refs_1_, bf16[128,512]{1,0:T(8,128)(2,1)} %get-tuple-element.12.refs_2_, ...), custom_call_target="tpu_custom_call" | custom-call | tf_op jit(solution)/shard_map/results/pallas_call | solution.py:561

commit v3 on v2

--- a/solution.py
+++ b/solution.py
@@ -26,9 +26,9 @@
     x_ref, q_ref, k_ref, v_ref, o_ref, doc_hbm,
     dq_out, dk_out, dv_out, wk_out, wv_out,
     qb, ob, kv, xb, acck, accv, lo_ref, dqs, t1s, tr1, t2s, tr2, gs, gb, pbuf, sdn, sup, rdn, rup, doc_ref, fin, precv,
-    a_send, a_kv, a_q, z_send, z_recv, s_send, s_recv, x_send, x_recv, xs_sem,
+    a_send, a_kv, a_q, z_send, z_recv, s_send, s_recv, x_send, x_recv, xs_send, xs_recv,
     dq_send, dq_recv, t1_sem, t2_sem, d_send, d_recv, f_send, dn_send, dn_recv, up_send, up_recv, doc_sem, out_sem, g_send, g_recv, p_sem,
-    xf_send, xf_recv,
+    xf_send, xf_recv, xg_send, xg_recv,
 ):
     seq = lax.axis_index("seq")
     head = lax.axis_index("head")
@@ -70,9 +70,10 @@
     across = dev(jnp.where(core == 0, down, up), i, 1 - core)
     flip = i + 1 - 2 * xh
     opposite = (z * 8 + flip, (1 - xl) * 2 + core)
-    for other in (sibling, above, below, across, opposite, dev(up, flip, core), dev(down, flip, core)):
+    beside = (seq, (1 - xl) * 2 + core)
+    for other in (sibling, above, below, across, opposite, beside, dev(up, flip, core), dev(down, flip, core)):
         pl.semaphore_signal(barrier, inc=1, device_id=other, device_id_type=MESH)
-    pl.semaphore_wait(barrier, 21)
+    pl.semaphore_wait(barrier, 22)
 
     def a_parts(l):
         row = pl.multiple_of(lane * T, T)
@@ -104,39 +105,78 @@
     a_start(0, 2)
     a_start(2, 4)
 
+    zs = pl.ds(4 * core, 4)
+    others = pl.ds(4 * (1 - core), 4)
+
     def x_part(yy, sub):
         row = 2 * yy + sub
         start = pl.multiple_of(84 * row - 4 * (row % 4), 16)
-        zs = pl.ds(4 * core, 4)
-        return x_ref.at[zs, pl.ds(start, 96), :], xb.at[sub, zs, :, pl.ds(pl.multiple_of(i * T, T), T)]
+        return x_ref.at[zs, pl.ds(start, 96), :], xb.at[sub, i, zs]
 
     def x_copy(step, sub):
         yy = lax.rem(y + step, 4)
         src, dst = x_part(yy, sub)
         return remote(src, dst, x_send.at[step, sub], x_recv.at[y, sub], dev(z, yy * 2 + xh, core))
 
+    def x_across_own():
+        src, dst = x_part(y, xl)
+        return remote(src, dst, xf_send.at[y], xf_recv.at[y], opposite)
+
+    def x_across(ys):
+        piece = xb.at[xl, ys * 2 + xh, zs]
+        return remote(piece, piece, xf_send.at[ys], xf_recv.at[ys], opposite)
+
+    def x_beside(ys):
+        piece = xb.at[1 - xl, ys * 2 + 1 - xh, zs]
+        return remote(piece, piece, xg_send.at[ys], xg_recv.at[ys], beside)
+
+    def xs_own(ys):
+        piece = xb.at[:, ys * 2 + xh, zs]
+        return remote(piece, piece, xs_send.at[ys, 0], xs_recv.at[ys, 0], sibling)
+
+    def xs_other(ys, s):
+        piece = xb.at[1 - xl if s == 0 else xl, ys * 2 + 1 - xh, zs]
+        return remote(piece, piece, xs_send.at[ys, 1 + s], xs_recv.at[ys, 1 + s], sibling)
+
+    def near_first(b):
+        return lax.rem(y + jnp.where(b < 2, b, 5 - b), 4)
+
     def x_start():
         for sub in range(2):
             src, dst = x_part(y, sub)
             pltpu.make_async_copy(src, dst, x_recv.at[y, sub]).start()
 
+        x_across_own().start()
+
         @pl.loop(1, 4)
-        def _(step):
+        def _(b):
             for sub in range(2):
-                x_copy(step, sub).start()
-
-    def x_tokens(j):
-        return pl.ds(pl.multiple_of(j * T, T), T)
-
-    def x_across(ys):
-        piece = xb.at[:, pl.ds(4 * core, 4), :, x_tokens(ys * 2 + xh)]
-        return remote(piece, piece, xf_send.at[ys], xf_recv.at[ys], opposite)
-
-    def x_forward(step):
-        ys = lax.rem(y + step, 4)
+                x_copy(jnp.where(b < 2, b, 5 - b), sub).start()
+
+    def x_arrived(ys):
         for sub in range(2):
-            got(xb.at[sub, pl.ds(4 * core, 4), :, x_tokens(ys * 2 + xh)], x_recv.at[ys, sub])
-        x_across(ys).start()
+            got(xb.at[sub, ys * 2 + xh, zs], x_recv.at[ys, sub])
+        xs_own(ys).start()
+
+    def x_second(b):
+        ys = near_first(b)
+        got(xb.at[1 - xl, ys * 2 + 1 - xh, zs], xf_recv.at[ys])
+        x_beside(ys).start()
+        xs_other(ys, 0).start()
+
+    def x_third(b):
+        ys = near_first(b)
+        got(xb.at[xl, ys * 2 + 1 - xh, zs], xg_recv.at[ys])
+        xs_other(ys, 1).start()
+
+    def x_complete():
+        @pl.loop(0, 4)
+        def _(ys):
+            got(xb.at[:, ys * 2 + xh, others], xs_recv.at[ys, 0])
+            got(xb.at[1 - xl, ys * 2 + 1 - xh, others], xs_recv.at[ys, 1])
+            got(xb.at[xl, ys * 2 + 1 - xh, others], xs_recv.at[ys, 2])
+
+    x_start()
 
     docs.wait()
     ids = doc_ref[pl.ds((2 * z + core) * 4, 4), :]
@@ -172,8 +212,6 @@
         def _():
             s_copy(m).start()
 
-    x_start()
-
     @pl.loop(0, 4)
     def _(m):
         z_copy(m).wait_recv()
@@ -204,7 +242,6 @@
         kk = kv[span, 0:T]
         vv = kv[span, T:2 * T]
         scores = dims(kk, q2, 1, 1)
-        x_forward(b)
         spot = lax.broadcasted_iota(jnp.int32, (SPAN, 2 * T), 0)
         low = lo_ref[pl.ds(b, 1), :] - b * T
         low = jnp.concatenate([low, low], 1)
@@ -244,6 +281,15 @@
         t1s[part] = total[512:1024, :].astype(BF16)
         t1_copy(part).start()
 
+    @pl.loop(1, 4)
+    def _(b):
+        ys = near_first(b)
+        x_arrived(ys)
+        x_across(ys).start()
+
+    x_arrived(y)
+    x_second(0)
+
     @pl.loop(0, 4)
     def _(b):
         t2_copy(b).wait_recv()
@@ -369,15 +415,10 @@
         gs[part] = (total[1024:1536, :] + tr1[part].astype(F32) + tr2[:, cols].astype(F32)).astype(BF16)
         first_send(part)
 
-    @pl.loop(0, 4)
-    def _(ys):
-        got(xb.at[:, pl.ds(4 * core, 4), :, x_tokens(ys * 2 + 1 - xh)], xf_recv.at[ys])
-
-    def xs_copy():
-        half = xb.at[:, pl.ds(4 * core, 4)]
-        return remote(half, half, xs_sem.at[0], xs_sem.at[1], sibling)
-
-    xs_copy().start()
+    @pl.loop(1, 4)
+    def _(b):
+        x_second(b)
+
 
     def dest(offset):
         return lax.rem(z + offset + NZ, NZ)
@@ -417,7 +458,7 @@
         @pl.loop(0, 4)
         def _(n):
             at = pl.ds((n % 2) * 4, 4)
-            lhs = xb[n // 2, at].reshape(384, 1024)
+            lhs = jnp.concatenate([xb[n // 2, j, at].reshape(384, T) for j in range(8)], 1)
             pbuf[part, n // 2, at] = jnp.dot(lhs, gb[part], preferred_element_type=F32).reshape(4, 96, 256)
 
     def p_copy(part):
@@ -446,8 +487,13 @@
     forward_side(1)
     token_send(0)
     token_send(1)
+
+    @pl.loop(0, 4)
+    def _(b):
+        x_third(b)
+
     gathered(0)
-    xs_copy().wait_recv()
+    x_complete()
     product(0)
     ring(0, 0)
     p_copy(0).start()
@@ -486,11 +532,14 @@
     def _(b):
         t2_copy(b).wait_send()
 
-    xs_copy().wait_send()
 
     @pl.loop(0, 4)
     def _(ys):
         x_across(ys).wait_send()
+        x_beside(ys).wait_send()
+        xs_own(ys).wait_send()
+        for s in range(2):
+            xs_other(ys, s).wait_send()
 
     @pl.loop(1, 4)
     def _(step):
@@ -541,7 +590,7 @@
         out_specs=(anywhere,) * 5,
         scratch_shapes=[
             vmem((512, 256), BF16), vmem((512, 256), BF16), vmem((WIN, 256), BF16),
-            vmem((2, 8, 96, 1024), BF16), vmem((WIN, T), F32), vmem((WIN, T), F32),
+            vmem((2, 8, 8, 96, T), BF16), vmem((WIN, T), F32), vmem((WIN, T), F32),
             vmem((8, T), jnp.int32), vmem((512, 256), BF16),
             vmem((2, 512, T), BF16), vmem((2, 512, T), BF16), vmem((512, 256), BF16), vmem((512, 256), BF16),
             vmem((2, 512, T), BF16), vmem((2, 1024, 256), BF16),
@@ -549,10 +598,10 @@
             vmem((2, 2, 2, 4, 48, 256), BF16), vmem((2, 2, 2, 3, 48, 256), BF16),
             vmem((2, 2, 2, 4, 48, 256), BF16), vmem((2, 2, 2, 3, 48, 256), BF16), vmem((64, 128), jnp.int32), vmem((2, 84, 512), F32),
             vmem((2, 96, 256), F32),
-            dma((4, 4)), dma((4, 2)), dma((4, 2)), dma((4,)), dma((4,)), dma((4,)), dma((4,)), dma((4, 2)), dma((4, 2)), dma((2,)),
+            dma((4, 4)), dma((4, 2)), dma((4, 2)), dma((4,)), dma((4,)), dma((4,)), dma((4,)), dma((4, 2)), dma((4, 2)), dma((4, 3)), dma((4, 3)),
             dma((4,)), dma((4,)), dma((2, 2)), dma((2, 4)), dma((2, 3, 2)), dma((2, 8)), dma((2, 8)),
             dma((2, 2, 2, 4)), dma((2, 2, 2, 4)), dma((2, 2, 2, 3)), dma((2, 2, 2, 3)), dma(()), dma((2,)), dma((2, 4)), dma((2, 4)),
-            dma((2, 2)), dma((4,)), dma((4,)),
+            dma((2, 2)), dma((4,)), dma((4,)), dma((4,)), dma((4,)),
         ],
         compiler_params=pltpu.CompilerParams(
             collective_id=0, has_side_effects=True, vmem_limit_bytes=60 << 20),

time: 80.1 us -> 75.9 us (0.948)
  the two profiles are of different devices: /device:TPU:20 before, /device:TPU:4 now
where the time goes in v3:
time: 75.9 us; the launch traced here: 74.8 us
  Pallas kernels  74.2 us (98%)
    pallas_call x1, Pallas kernels, local(): pl.pallas_call(kernel, name='window_backward', out_shape=outs, in_specs=[...  72.2 us
    pallas_call x1, Pallas kernels, local(): pl.pallas_call(copies, name='results', out_shape=outs, in_specs=[anywhere...  1.95 us

profile of v3, /device:TPU:4, one launch (start us, length us, event | category | flops | bytes accessed | tf_op | source)
XLA Modules:
  0.0 74.8 jit_solution(12757910353710224070)
XLA Ops:
  0.6 72.2 %window_backward.1 = (bf16[128,1024]{1,0:T(8,128)(2,1)}, bf16[128,512]{1,0:T(8,128)(2,1)}, bf16[128,512]{1,0:T(8,128)(2,1)}, f32[84,512]{1,0:T(8,128)}, f32[84,512]{1,0:T(8,128)}) custom-call(bf16[8,672,128]{2,1,0:T(8,128)(2,1)} %bitcast.2, bf16[128,1024]{1,0:T(8,128)(2,1)} %q_ref.1, bf16[128,512]{1,0:T(8,128)(2,1)} %k_ref.1, bf16[128,512]{1,0:T(8,128)(2,1)} %v_ref.1, ...), custom_call_target="tpu_custom_call" | custom-call | flops 3000000000 | bytes 12000000 | tf_op jit(solution)/shard_map/window_backward/pallas_call | solution.py:585
  72.8 1.9 %results.1 = (bf16[128,1024]{1,0:T(8,128)(2,1)}, bf16[128,512]{1,0:T(8,128)(2,1)}, bf16[128,512]{1,0:T(8,128)(2,1)}, f32[84,512]{1,0:T(8,128)}, f32[84,512]{1,0:T(8,128)}) custom-call(bf16[128,1024]{1,0:T(8,128)(2,1)} %get-tuple-element.10.refs_0_, bf16[128,512]{1,0:T(8,128)(2,1)} %get-tuple-element.11.refs_1_, bf16[128,512]{1,0:T(8,128)(2,1)} %get-tuple-element.12.refs_2_, ...), custom_call_target="tpu_custom_call" | custom-call | tf_op jit(solution)/shard_map/results/pallas_call | solution.py:610

commit v4 on v3

--- a/solution.py
+++ b/solution.py
@@ -25,7 +25,7 @@
 def kernel(
     x_ref, q_ref, k_ref, v_ref, o_ref, doc_hbm,
     dq_out, dk_out, dv_out, wk_out, wv_out,
-    qb, ob, kv, xb, acck, accv, lo_ref, dqs, t1s, tr1, t2s, tr2, gs, gb, pbuf, sdn, sup, rdn, rup, doc_ref, fin, precv,
+    qb, ob, kv, xb, acck, accv, lo_ref, dqs, t1s, tr1, t2s, tr2, gs, gb, pbuf, sdn, sup, rdn, rup, doc_ref, fin, precv, sbuf, gbuf,
     a_send, a_kv, a_q, z_send, z_recv, s_send, s_recv, x_send, x_recv, xs_send, xs_recv,
     dq_send, dq_recv, t1_sem, t2_sem, d_send, d_recv, f_send, dn_send, dn_recv, up_send, up_recv, doc_sem, out_sem, g_send, g_recv, p_sem,
     xf_send, xf_recv, xg_send, xg_recv,
@@ -69,11 +69,19 @@
 
     across = dev(jnp.where(core == 0, down, up), i, 1 - core)
     flip = i + 1 - 2 * xh
-    opposite = (z * 8 + flip, (1 - xl) * 2 + core)
+
+    def opposite(yy):
+        return (z * 8 + yy * 2 + 1 - xh, (1 - xl) * 2 + core)
+
     beside = (seq, (1 - xl) * 2 + core)
-    for other in (sibling, above, below, across, opposite, beside, dev(up, flip, core), dev(down, flip, core)):
+    for other in (sibling, above, below, across, beside, dev(up, flip, core), dev(down, flip, core)):
         pl.semaphore_signal(barrier, inc=1, device_id=other, device_id_type=MESH)
-    pl.semaphore_wait(barrier, 22)
+
+    @pl.loop(0, 4)
+    def _(yy):
+        pl.semaphore_signal(barrier, inc=1, device_id=opposite(yy), device_id_type=MESH)
+
+    pl.semaphore_wait(barrier, 25)
 
     def a_parts(l):
         row = pl.multiple_of(lane * T, T)
@@ -118,13 +126,10 @@
         src, dst = x_part(yy, sub)
         return remote(src, dst, x_send.at[step, sub], x_recv.at[y, sub], dev(z, yy * 2 + xh, core))
 
-    def x_across_own():
-        src, dst = x_part(y, xl)
-        return remote(src, dst, xf_send.at[y], xf_recv.at[y], opposite)
-
-    def x_across(ys):
-        piece = xb.at[xl, ys * 2 + xh, zs]
-        return remote(piece, piece, xf_send.at[ys], xf_recv.at[ys], opposite)
+    def x_across(step):
+        yy = lax.rem(y + step, 4)
+        src, dst = x_part(yy, xl)
+        return remote(src, dst, xf_send.at[step], xf_recv.at[y], opposite(yy))
 
     def x_beside(ys):
         piece = xb.at[1 - xl, ys * 2 + 1 - xh, zs]
@@ -146,7 +151,9 @@
             src, dst = x_part(y, sub)
             pltpu.make_async_copy(src, dst, x_recv.at[y, sub]).start()
 
-        x_across_own().start()
+        @pl.loop(0, 4)
+        def _(b):
+            x_across(jnp.where(b < 2, b, 5 - b)).start()
 
         @pl.loop(1, 4)
         def _(b):
@@ -175,8 +182,6 @@
             got(xb.at[:, ys * 2 + xh, others], xs_recv.at[ys, 0])
             got(xb.at[1 - xl, ys * 2 + 1 - xh, others], xs_recv.at[ys, 1])
             got(xb.at[xl, ys * 2 + 1 - xh, others], xs_recv.at[ys, 2])
-
-    x_start()
 
     docs.wait()
     ids = doc_ref[pl.ds((2 * z + core) * 4, 4), :]
@@ -212,6 +217,8 @@
         def _():
             s_copy(m).start()
 
+    x_start()
+
     @pl.loop(0, 4)
     def _(m):
         z_copy(m).wait_recv()
@@ -233,32 +240,41 @@
         col = pl.ds(pl.multiple_of(lane * 2 * T, 2 * T), 2 * T)
         return dqs.at[rows(0, m)], dq_out.at[:, col], dq_send.at[m], dq_recv.at[lane], dev(z, 4 * core + m, own_half)
 
-    @pl.loop(0, 4)
-    def _(b):
-        here = rows(0, b)
-        span = pl.ds(pl.multiple_of(b * T, T), SPAN)
-        q2 = jnp.concatenate([qb[here, 0:T], qb[here, T:2 * T]], 0)
-        o2 = jnp.concatenate([ob[here, 0:T], ob[here, T:2 * T]], 0)
-        kk = kv[span, 0:T]
-        vv = kv[span, T:2 * T]
-        scores = dims(kk, q2, 1, 1)
-        spot = lax.broadcasted_iota(jnp.int32, (SPAN, 2 * T), 0)
-        low = lo_ref[pl.ds(b, 1), :] - b * T
+    def pair(ref, b):
+        return jnp.concatenate([ref[b * T:(b + 1) * T, 0:T], ref[b * T:(b + 1) * T, T:2 * T]], 0)
+
+    def first_products(b):
+        sbuf[b % 2] = dims(kv[b * T:b * T + SPAN, 0:T], pair(qb, b), 1, 1)
+        gbuf[b % 2] = dims(kv[b * T:b * T + SPAN, T:2 * T], pair(ob, b), 1, 1)
+
+    spot = lax.broadcasted_iota(jnp.int32, (1024, 2 * T), 0)
+    tail = lax.broadcasted_iota(jnp.int32, (T, 2 * T), 0) + 1024
+    high = 1024 + lax.broadcasted_iota(jnp.int32, (1, 2 * T), 1) % T
+    first_products(0)
+    for b in range(4):
+        here = slice(b * T, (b + 1) * T)
+        span = slice(b * T, b * T + SPAN)
+        if b == 1:
+            x_second(0)
+        if b < 3:
+            first_products(b + 1)
+        low = lo_ref[b:b + 1, :] - b * T
         low = jnp.concatenate([low, low], 1)
-        high = 1024 + lax.broadcasted_iota(jnp.int32, (1, 2 * T), 1) % T
-        scores = jnp.where((spot >= low) & (spot <= high), scores, NEG)
+        scores = jnp.concatenate([
+            jnp.where(spot >= low, sbuf[b % 2, 0:1024], NEG),
+            jnp.where((tail >= low) & (tail <= high), sbuf[b % 2, 1024:SPAN], NEG)], 0)
         top = jnp.max(scores, axis=0, keepdims=True)
         expo = jnp.exp2((scores - top) * (SCALE * LOG2E))
         probs = expo * (1.0 / jnp.sum(expo, axis=0, keepdims=True))
-        grad_probs = dims(vv, o2, 1, 1)
+        grad_probs = gbuf[b % 2]
         delta = jnp.sum(probs * grad_probs, axis=0, keepdims=True)
         grad_scores = (SCALE * probs * (grad_probs - delta)).astype(BF16)
-        accv[span, :] += dims(probs.astype(BF16), o2, 1, 0)
-        acck[span, :] += dims(grad_scores, q2, 1, 0)
+        accv[span, :] += dims(probs.astype(BF16), pair(ob, b), 1, 0)
+        acck[span, :] += dims(grad_scores, pair(qb, b), 1, 0)
         t2s[here, 0:T] = acck[here, :].astype(BF16)
         t2s[here, T:2 * T] = accv[here, :].astype(BF16)
         t2_copy(b).start()
-        dq2 = dims(grad_scores, kk, 0, 0).astype(BF16)
+        dq2 = dims(grad_scores, kv[span, 0:T], 0, 0).astype(BF16)
         dqs[here, 0:T] = dq2[:T]
         dqs[here, T:2 * T] = dq2[T:]
         mine = self_a & (b == lane)
@@ -283,12 +299,11 @@
 
     @pl.loop(1, 4)
     def _(b):
-        ys = near_first(b)
-        x_arrived(ys)
-        x_across(ys).start()
-
-    x_arrived(y)
-    x_second(0)
+        x_second(b)
+
+    @pl.loop(0, 4)
+    def _(b):
+        x_arrived(near_first(b))
 
     @pl.loop(0, 4)
     def _(b):
@@ -414,10 +429,6 @@
         cols = pl.ds((1 - part) * T, T)
         gs[part] = (total[1024:1536, :] + tr1[part].astype(F32) + tr2[:, cols].astype(F32)).astype(BF16)
         first_send(part)
-
-    @pl.loop(1, 4)
-    def _(b):
-        x_second(b)
 
 
     def dest(offset):
@@ -597,7 +608,7 @@
             vmem((2, 2, 8, 96, 256), F32),
             vmem((2, 2, 2, 4, 48, 256), BF16), vmem((2, 2, 2, 3, 48, 256), BF16),
             vmem((2, 2, 2, 4, 48, 256), BF16), vmem((2, 2, 2, 3, 48, 256), BF16), vmem((64, 128), jnp.int32), vmem((2, 84, 512), F32),
-            vmem((2, 96, 256), F32),
+            vmem((2, 96, 256), F32), vmem((2, SPAN, 256), F32), vmem((2, SPAN, 256), F32),
             dma((4, 4)), dma((4, 2)), dma((4, 2)), dma((4,)), dma((4,)), dma((4,)), dma((4,)), dma((4, 2)), dma((4, 2)), dma((4, 3)), dma((4, 3)),
             dma((4,)), dma((4,)), dma((2, 2)), dma((2, 4)), dma((2, 3, 2)), dma((2, 8)), dma((2, 8)),
             dma((2, 2, 2, 4)), dma((2, 2, 2, 4)), dma((2, 2, 2, 3)), dma((2, 2, 2, 3)), dma(()), dma((2,)), dma((2, 4)), dma((2, 4)),

time: 75.9 us -> 74.4 us (0.980); the launches traced: 74.8 us -> 74.2 us
  no operation moved by 1% of the time
where the time goes in v4:
time: 74.4 us; the launch traced here: 74.2 us
  Pallas kernels  73.6 us (99%)
    pallas_call x1, Pallas kernels, local(): pl.pallas_call(kernel, name='window_backward', out_shape=outs, in_specs=[...  71.6 us
    pallas_call x1, Pallas kernels, local(): pl.pallas_call(copies, name='results', out_shape=outs, in_specs=[anywhere...  1.95 us

profile of v4, /device:TPU:4, one launch (start us, length us, event | category | flops | bytes accessed | tf_op | source)
XLA Modules:
  0.0 74.2 jit_solution(10846391347236685527)
XLA Ops:
  0.6 71.6 %window_backward.1 = (bf16[128,1024]{1,0:T(8,128)(2,1)}, bf16[128,512]{1,0:T(8,128)(2,1)}, bf16[128,512]{1,0:T(8,128)(2,1)}, f32[84,512]{1,0:T(8,128)}, f32[84,512]{1,0:T(8,128)}) custom-call(bf16[8,672,128]{2,1,0:T(8,128)(2,1)} %bitcast.2, bf16[128,1024]{1,0:T(8,128)(2,1)} %q_ref.1, bf16[128,512]{1,0:T(8,128)(2,1)} %k_ref.1, bf16[128,512]{1,0:T(8,128)(2,1)} %v_ref.1, ...), custom_call_target="tpu_custom_call" | custom-call | flops 3000000000 | bytes 12000000 | tf_op jit(solution)/shard_map/window_backward/pallas_call | solution.py:596
  72.3 1.9 %results.1 = (bf16[128,1024]{1,0:T(8,128)(2,1)}, bf16[128,512]{1,0:T(8,128)(2,1)}, bf16[128,512]{1,0:T(8,128)(2,1)}, f32[84,512]{1,0:T(8,128)}, f32[84,512]{1,0:T(8,128)}) custom-call(bf16[128,1024]{1,0:T(8,128)(2,1)} %get-tuple-element.10.refs_0_, bf16[128,512]{1,0:T(8,128)(2,1)} %get-tuple-element.11.refs_1_, bf16[128,512]{1,0:T(8,128)(2,1)} %get-tuple-element.12.refs_2_, ...), custom_call_target="tpu_custom_call" | custom-call | tf_op jit(solution)/shard_map/results/pallas_call | solution.py:621

commit v5 on v4

--- a/solution.py
+++ b/solution.py
@@ -277,16 +277,6 @@
         dq2 = dims(grad_scores, kv[span, 0:T], 0, 0).astype(BF16)
         dqs[here, 0:T] = dq2[:T]
         dqs[here, T:2 * T] = dq2[T:]
-        mine = self_a & (b == lane)
-        src, dst, ssem, rsem, to = dq_copy(b)
-
-        @pl.when(mine)
-        def _():
-            pltpu.make_async_copy(src, dst, rsem).start()
-
-        @pl.when(jnp.logical_not(mine))
-        def _():
-            remote(src, dst, ssem, rsem, to).start()
 
     owner = dev(jnp.where(core == 0, down, z), i, 1 - core)
 
@@ -496,8 +486,6 @@
 
     forward_side(0)
     forward_side(1)
-    token_send(0)
-    token_send(1)
 
     @pl.loop(0, 4)
     def _(b):
@@ -508,15 +496,30 @@
     product(0)
     ring(0, 0)
     p_copy(0).start()
-    ring(0, 1)
+    @pl.loop(0, 4)
+    def _(b):
+        mine = self_a & (b == lane)
+        src, dst, ssem, rsem, to = dq_copy(b)
+
+        @pl.when(mine)
+        def _():
+            pltpu.make_async_copy(src, dst, rsem).start()
+
+        @pl.when(jnp.logical_not(mine))
+        def _():
+            remote(src, dst, ssem, rsem, to).start()
+
+    token_send(0)
+    token_send(1)
     gathered(1)
     product(1)
     ring(1, 0)
     p_copy(1).start()
+    ring(0, 1)
+    ring(1, 1)
     ring(0, 2)
-    ring(1, 1)
+    ring(1, 2)
     ring(0, 3)
-    ring(1, 2)
     ring(1, 3)
     finish(0)
     finish(1)

time: 74.4 us -> 68.5 us (0.921)
  Pallas kernels: 73.6 us -> 67.4 us
    pallas_call x1, Pallas kernels: 71.6 us -> 65.4 us  [local(): pl.pallas_call(kernel, name='window_backward', out_shape=outs, in_specs=[...]
where the time goes in v5:
time: 68.5 us; the launch traced here: 68 us
  Pallas kernels  67.4 us (98%)
    pallas_call x1, Pallas kernels, local(): pl.pallas_call(kernel, name='window_backward', out_shape=outs, in_specs=[...  65.4 us
    pallas_call x1, Pallas kernels, local(): pl.pallas_call(copies, name='results', out_shape=outs, in_specs=[anywhere...  1.95 us

profile of v5, /device:TPU:4, one launch (start us, length us, event | category | flops | bytes accessed | tf_op | source)
XLA Modules:
  0.0 68.0 jit_solution(17505386134835699673)
XLA Ops:
  0.6 65.4 %window_backward.1 = (bf16[128,1024]{1,0:T(8,128)(2,1)}, bf16[128,512]{1,0:T(8,128)(2,1)}, bf16[128,512]{1,0:T(8,128)(2,1)}, f32[84,512]{1,0:T(8,128)}, f32[84,512]{1,0:T(8,128)}) custom-call(bf16[8,672,128]{2,1,0:T(8,128)(2,1)} %bitcast.2, bf16[128,1024]{1,0:T(8,128)(2,1)} %q_ref.1, bf16[128,512]{1,0:T(8,128)(2,1)} %k_ref.1, bf16[128,512]{1,0:T(8,128)(2,1)} %v_ref.1, ...), custom_call_target="tpu_custom_call" | custom-call | flops 3000000000 | bytes 12000000 | tf_op jit(solution)/shard_map/window_backward/pallas_call | solution.py:599
  66.0 1.9 %results.1 = (bf16[128,1024]{1,0:T(8,128)(2,1)}, bf16[128,512]{1,0:T(8,128)(2,1)}, bf16[128,512]{1,0:T(8,128)(2,1)}, f32[84,512]{1,0:T(8,128)}, f32[84,512]{1,0:T(8,128)}) custom-call(bf16[128,1024]{1,0:T(8,128)(2,1)} %get-tuple-element.10.refs_0_, bf16[128,512]{1,0:T(8,128)(2,1)} %get-tuple-element.11.refs_1_, bf16[128,512]{1,0:T(8,128)(2,1)} %get-tuple-element.12.refs_2_, ...), custom_call_target="tpu_custom_call" | custom-call | tf_op jit(solution)/shard_map/results/pallas_call | solution.py:624
